TPU v7x, 256 devices: a whole 4x4x8 slice. The times are simulated.
256 devices in a mesh: cuts: 64 (over y_lo, z, x), dom: 4 (over y_hi, core).
Axes of the slice: x: 4, y: 4 (y_hi: 2, y_lo: 2; y = y_hi * 2 + y_lo), z: 8, core: 2. Of those that a mesh axis runs over, the one named last changes fastest.
Arguments:
- particles: float32 [2, 5, 64, 65536], P(None, None, 'cuts', 'dom'), may hold values from -5 to 5, as said below
- cells: int32 [2, 64, 65536], P(None, 'cuts', 'dom'), may hold values from 0 to 16383
- counts: int32 [2, 2, 64, 4], P(None, None, 'cuts', 'dom'), may hold values from 0 to 4096, as said below
Outputs:
- kept: float32 [2, 5, 64, 65536], P(None, None, 'cuts', 'dom')
- arrivals: float32 [2, 5, 64, 32768], P(None, None, 'cuts', 'dom')
Inputs may be any that keep to these rules, and one draw needn't show every extreme that they name: `particles`: components 0 to 3 are coordinates; component 4 is a positive weight between 0.25 and 4. `counts`: each count is at most 4096, and some count equals 4096.
All inputs are finite; a program needn't handle non-finite values.
Results may differ from a plain program's by a relative error of at most 0.00025.
Values sent between devices are 32-bit elements; how exact they have to be, the bound alone decides.
A program may use at most 64 MiB of HBM per device.

v0:
```python
import math

import jax
import jax.numpy as jnp
from jax import lax
from jax.sharding import PartitionSpec as P

GRID = 128
SECTIONS = 3


KICK_SCALE = 0.01
ADJUST_X = 0.31
ADJUST_Y = 0.32


def from_behind(block, axis, distance):
    devices = range(lax.axis_size(axis))
    route = [((i - distance) % len(devices), i) for i in devices]
    return lax.ppermute(block, axis, route)


def from_behind_2(value, axis, steps):
    count = lax.axis_size(axis)
    first, last = (max(0, -steps), min(count, count - steps))
    return lax.ppermute(value, axis, [(source, source + steps) for source in range(first, last)])


def sine_basis(grid_size):
    index = jnp.arange(grid_size, dtype=jnp.int32) + 1
    product = index[:, None] * index[None, :] % (2 * (grid_size + 1))
    angle = product.astype(jnp.float32) * (math.pi / (grid_size + 1))
    basis = math.sqrt(2.0 / (grid_size + 1)) * jnp.sin(angle)
    eigen = 2.0 - 2.0 * jnp.cos(index.astype(jnp.float32) * (math.pi / (grid_size + 1)))
    return (basis, eigen[:, None] + eigen[None, :])


def solve_potential(density, basis, eigen_sum):
    highest = lax.Precision.HIGHEST
    spectrum = jnp.dot(
        jnp.dot(basis, density, precision=highest, preferred_element_type=jnp.float32),
        basis,
        precision=highest,
        preferred_element_type=jnp.float32,
    )
    inner = jnp.dot(
        basis, spectrum / eigen_sum, precision=highest, preferred_element_type=jnp.float32
    )
    return jnp.dot(inner, basis, precision=highest, preferred_element_type=jnp.float32)


def differences(potential):
    padded = jnp.pad(potential, 1)
    field_x = (padded[:-2, 1:-1] - padded[2:, 1:-1]) * 0.5
    field_y = (padded[1:-1, :-2] - padded[1:-1, 2:]) * 0.5
    return jnp.concatenate([field_x, field_y], axis=1)


def deposit(row_index, col_index, weights, grid_size):
    block_size = min(row_index.shape[0], 1024)
    blocks = row_index.shape[0] // block_size
    levels = jnp.arange(grid_size, dtype=jnp.int32)

    def accumulate(running, pieces):
        row_part, col_part, weight_part = pieces
        onehot_rows = (row_part[:, None] == levels[None, :]).astype(jnp.float32)
        weighted_cols = jnp.where(col_part[:, None] == levels[None, :], weight_part[:, None], 0.0)
        term = lax.dot_general(
            onehot_rows,
            weighted_cols,
            (((0,), (0,)), ((), ())),
            precision=lax.Precision.HIGHEST,
            preferred_element_type=jnp.float32,
        )
        return (running + term, None)

    start = jnp.zeros((grid_size, grid_size), jnp.float32)
    pieces = (
        row_index.reshape(blocks, block_size),
        col_index.reshape(blocks, block_size),
        weights.reshape(blocks, block_size),
    )
    running, unused = lax.scan(accumulate, start, pieces)
    return running


def lookup(field, row_index, col_index):
    grid_size = field.shape[0]
    block_size = min(row_index.shape[0], 1024)
    blocks = row_index.shape[0] // block_size
    levels = jnp.arange(grid_size, dtype=jnp.int32)

    def one_block(pieces):
        row_part, col_part = pieces
        onehot_rows = (row_part[:, None] == levels[None, :]).astype(jnp.float32)
        picked = jnp.dot(
            onehot_rows, field, precision=lax.Precision.HIGHEST, preferred_element_type=jnp.float32
        )
        onehot_cols = (col_part[:, None] == levels[None, :]).astype(jnp.float32)
        value_x = jnp.sum(picked[:, :grid_size] * onehot_cols, axis=1)
        value_y = jnp.sum(picked[:, grid_size:] * onehot_cols, axis=1)
        return (value_x, value_y)

    value_x, value_y = lax.map(
        one_block, (row_index.reshape(blocks, block_size), col_index.reshape(blocks, block_size))
    )
    return (value_x.reshape(-1), value_y.reshape(-1))


def local(particles, cells, counts):
    state = particles[:, :, 0, :]
    cell_local = cells[:, 0, :]
    grid_size = GRID
    row_index = cell_local // grid_size
    col_index = cell_local % grid_size
    partial_value = jnp.stack(
        [
            deposit(row_index[beam_no], col_index[beam_no], state[beam_no, 4], grid_size)
            for beam_no in range(2)
        ],
        axis=0,
    )
    density = lax.psum(partial_value, "dom")
    basis, eigen_sum = sine_basis(grid_size)
    potentials = [solve_potential(density[beam_no], basis, eigen_sum) for beam_no in range(2)]
    outgoing = [differences(potentials[beam_no]) for beam_no in range(2)]
    ahead_held = outgoing[1]
    behind_held = outgoing[0]
    ahead_total = jnp.zeros_like(outgoing[1])
    behind_total = jnp.zeros_like(outgoing[0])
    for section_num in range(1, SECTIONS + 1):
        ahead_held = from_behind(ahead_held, "cuts", -1)
        behind_held = from_behind(behind_held, "cuts", 1)
        ahead_total = ahead_total + ahead_held
        behind_total = behind_total + behind_held
    mom_x = [state[0, 1], state[1, 1]]
    mom_y = [state[0, 3], state[1, 3]]
    kick_x, kick_y = lookup(ahead_total, row_index[0], col_index[0])
    mom_x[0] = mom_x[0] + KICK_SCALE * kick_x
    mom_y[0] = mom_y[0] + KICK_SCALE * kick_y
    kick_x, kick_y = lookup(behind_total, row_index[1], col_index[1])
    mom_x[1] = mom_x[1] + KICK_SCALE * kick_x
    mom_y[1] = mom_y[1] + KICK_SCALE * kick_y
    cos_x, sin_x = (math.cos(2 * math.pi * ADJUST_X), math.sin(2 * math.pi * ADJUST_X))
    cos_y, sin_y = (math.cos(2 * math.pi * ADJUST_Y), math.sin(2 * math.pi * ADJUST_Y))
    beams_out = []
    for beam_no in range(2):
        pos_x = state[beam_no, 0]
        pos_y = state[beam_no, 2]
        new_x = cos_x * pos_x + sin_x * mom_x[beam_no]
        new_px = -sin_x * pos_x + cos_x * mom_x[beam_no]
        new_y = cos_y * pos_y + sin_y * mom_y[beam_no]
        new_py = -sin_y * pos_y + cos_y * mom_y[beam_no]
        beams_out.append(jnp.stack([new_x, new_px, new_y, new_py, state[beam_no, 4]], axis=0))
    final_state = jnp.stack(beams_out, axis=0)
    length = final_state.shape[-1]
    capacity = length // 4
    up_count = counts[:, 0, 0, 0]
    down_count = counts[:, 1, 0, 0]
    slot_index = lax.iota(jnp.int32, length)
    leaving = (slot_index[None, :] >= length - up_count[:, None]) | (
        slot_index[None, :] < down_count[:, None]
    )
    kept_state = jnp.where(leaving[:, None, :], 0.0, final_state)
    block_slot = lax.iota(jnp.int32, capacity)
    up_block = jnp.where(
        (block_slot[None, :] < up_count[:, None])[:, None, :],
        final_state[:, :, length - capacity :][:, :, ::-1],
        0.0,
    )
    down_block = jnp.where(
        (block_slot[None, :] < down_count[:, None])[:, None, :], final_state[:, :, :capacity], 0.0
    )
    from_below = from_behind_2(up_block, "cuts", 1)
    from_above = from_behind_2(down_block, "cuts", -1)
    arrivals = jnp.concatenate([from_below, from_above], axis=-1)
    return (kept_state[:, :, None, :], arrivals[:, :, None, :])


def solution(mesh):
    return jax.shard_map(
        local,
        mesh=mesh,
        in_specs=(
            P(None, None, "cuts", "dom"),
            P(None, "cuts", "dom"),
            P(None, None, "cuts", "dom"),
        ),
        out_specs=(P(None, None, "cuts", "dom"), P(None, None, "cuts", "dom")),
        check_vma=False,
    )
```

profile of v0, /device:TPU:8, one launch (start us, length us, event | category | flops | bytes accessed | tf_op | source)
XLA Modules:
  0.0 187.8 jit_solution(10523047190586749882)
XLA Ops:
  7.2 1.4 and_select_fusion
  10.3 18.7 %while.54 = (s32[]{:T(128)}, f32[128,128]{1,0:T(8,128)S(1)}, s32[16,1024]{1,0:T(8,128)S(1)}, s32[16,1024]{1,0:T(8,128)S(1)}, f32[16,1024]{1,0:T(8,128)S(1)}, /*index=5*/s32[]{:T(128)}, s32[]{:T(128)}) while((s32[]{:T(128)}, f32[128,128]{1,0:T(8,128)S(1)}, s32[16,1024]{1,0:T(8,128)S(1)}, s32[16,1024]{1,0:T(8,128)S(1)}, ...), condition=%wide.region_1.2_spmd.clone.clone, body=%wide.region_0.1_spmd.clone.clone.sunk | while | flops 201752576 | bytes 168031 | solution.py:83
  13.8 1.1 convolution_add_fusion.4
  15.0 1.1 convolution_add_fusion.4
  22.0 1.1 convolution_add_fusion.4
  23.2 1.1 convolution_add_fusion.4
  29.0 18.7 %while.55 = (s32[]{:T(128)}, f32[128,128]{1,0:T(8,128)S(1)}, s32[16,1024]{1,0:T(8,128)S(1)}, s32[16,1024]{1,0:T(8,128)S(1)}, f32[16,1024]{1,0:T(8,128)S(1)}, /*index=5*/s32[]{:T(128)}, s32[]{:T(128)}) while((s32[]{:T(128)}, f32[128,128]{1,0:T(8,128)S(1)}, s32[16,1024]{1,0:T(8,128)S(1)}, s32[16,1024]{1,0:T(8,128)S(1)}, ...), condition=%wide.region_3.4_spmd.clone.clone, body=%wide.region_2.3_spmd.clone.clone.sunk | while | flops 201752576 | bytes 168031 | solution.py:83
  29.1 1.1 convolution_add_fusion.5
  38.4 1.1 convolution_add_fusion.5
  49.3 46.5 %all-reduce.4.cloned.1.call-done = f32[2,128,128]{2,1,0:T(8,128)} async-done(((f32[2,128,128]{2,1,0:T(8,128)}), f32[2,128,128]{2,1,0:T(8,128)}) %all-reduce.4.cloned.1.call-update) | async-done | bytes 131088 | tf_op jit(solution)/shard_map/psum | solution.py:123
  95.8 1.4 fusion.46
  99.0 1.5 collective-permute-start.3
  102.8 5.7 %collective-permute-start = (f32[128,256]{0,1:T(8,128)S(1)}, f32[128,256]{0,1:T(8,128)S(1)}, u32[]{:S(2)}, u32[]{:S(2)}) collective-permute-start(f32[128,256]{0,1:T(8,128)S(1)} %pad_maximum_fusion.3), channel_id=1, source_target_pairs={{4,0},{8,4},{12,8},{16,12},{20,16},{24,20},{28,24},{32,28},{36,32}... | collective-permute-start | bytes 393224 | tf_op jit(solution)/shard_map/ppermute | solution.py:20
  109.6 2.3 %collective-permute-done = f32[128,256]{0,1:T(8,128)S(1)} collective-permute-done((f32[128,256]{0,1:T(8,128)S(1)}, f32[128,256]{0,1:T(8,128)S(1)}, u32[]{:S(2)}, u32[]{:S(2)}) %collective-permute-start) | collective-permute-done | bytes 131104 | tf_op jit(solution)/shard_map/ppermute | solution.py:20
  111.8 6.7 %collective-permute-start.1 = (f32[128,256]{0,1:T(8,128)S(1)}, f32[128,256]{0,1:T(8,128)S(1)}, u32[]{:S(2)}, u32[]{:S(2)}) collective-permute-start(f32[128,256]{0,1:T(8,128)S(1)} %collective-permute-done), channel_id=1, source_target_pairs={{4,0},{8,4},{12,8},{16,12},{20,16},{24,20},{28,24},{32,28},{36,32}... | collective-permute-start | bytes 393224 | tf_op jit(solution)/shard_map/ppermute | solution.py:20
  119.0 2.1 %collective-permute-done.1 = f32[128,256]{0,1:T(8,128)S(1)} collective-permute-done((f32[128,256]{0,1:T(8,128)S(1)}, f32[128,256]{0,1:T(8,128)S(1)}, u32[]{:S(2)}, u32[]{:S(2)}) %collective-permute-start.1) | collective-permute-done | bytes 131104 | tf_op jit(solution)/shard_map/ppermute | solution.py:20
  121.0 6.7 %collective-permute-start.2 = (f32[128,256]{0,1:T(8,128)S(1)}, f32[128,256]{0,1:T(8,128)S(1)}, u32[]{:S(2)}, u32[]{:S(2)}) collective-permute-start(f32[128,256]{0,1:T(8,128)S(1)} %collective-permute-done.1), channel_id=1, source_target_pairs={{4,0},{8,4},{12,8},{16,12},{20,16},{24,20},{28,24},{32,28},{36,32}... | collective-permute-start | bytes 393224 | tf_op jit(solution)/shard_map/ppermute | solution.py:20
  128.2 16.2 %while.53 = (s32[]{:T(128)}, f32[16,1024]{1,0:T(8,128)S(1)}, f32[16,1024]{1,0:T(8,128)S(1)}, s32[16,1024]{1,0:T(8,128)S(1)}, s32[16,1024]{1,0:T(8,128)S(1)}, /*index=5*/f32[128,256]{1,0:T(8,128)S(1)}, s32[]{:T(128)}, s32[]{:T(128)}) while((s32[]{:T(128)}, f32[16,1024]{1,0:T(8,128)S(1)}, f32[16,1024]{1,0:T(8,128)S(1)}, ...), condition=%wide.region_12.13_spmd.clone.clone, body=%wide.region_9.12_spmd.clone.clone.sunk | while | flops 403437568 | bytes 2277473 | solution.py:104
  144.8 16.2 %while.52 = (s32[]{:T(128)}, f32[16,1024]{1,0:T(8,128)S(1)}, f32[16,1024]{1,0:T(8,128)S(1)}, s32[16,1024]{1,0:T(8,128)S(1)}, s32[16,1024]{1,0:T(8,128)S(1)}, /*index=5*/f32[128,256]{1,0:T(8,128)S(1)}, s32[]{:T(128)}, s32[]{:T(128)}) while((s32[]{:T(128)}, f32[16,1024]{1,0:T(8,128)S(1)}, f32[16,1024]{1,0:T(8,128)S(1)}, ...), condition=%wide.region_8.9_spmd.clone.clone, body=%wide.region_5.8_spmd.clone.clone.sunk | while | flops 403437568 | bytes 2277473 | solution.py:104
  163.5 2.3 %rev.3 = f32[2,5,4096]{2,1,0:T(8,128)S(1)} reverse(f32[2,5,4096]{2,1,0:T(8,128)S(1)} %get-tuple-element.388), dimensions={2} | reverse | bytes 327680 | tf_op jit(solution)/shard_map/rev | solution.py:168
  165.9 1.9 %collective-permute-start.6 = (f32[2,5,4096]{2,1,0:T(8,128)S(1)}, f32[2,5,4096]{2,1,0:T(8,128)S(1)}, u32[]{:S(2)}, u32[]{:S(2)}) collective-permute-start(f32[2,5,4096]{2,1,0:T(8,128)S(1)} %broadcast_select_fusion.1), channel_id=1, source_target_pairs={{0,4},{4,8},{8,12},{12,16},{16,20},{20,24},{24,28},{28,32},{32,36}... | collective-permute-start | bytes 491528 | tf_op jit(solution)/shard_map/ppermute | solution.py:26
  167.8 8.1 %collective-permute-start.7 = (f32[2,5,4096]{2,1,0:T(8,128)S(1)}, f32[2,5,4096]{2,1,0:T(8,128)S(1)}, u32[]{:S(2)}, u32[]{:S(2)}) collective-permute-start(f32[2,5,4096]{2,1,0:T(8,128)S(1)} %get-tuple-element.389), channel_id=1, source_target_pairs={{4,0},{8,4},{12,8},{16,12},{20,16},{24,20},{28,24},{32,28},{36,32}... | collective-permute-start | bytes 491528 | tf_op jit(solution)/shard_map/ppermute | solution.py:26
  176.3 1.6 broadcast_select_fusion
  178.4 1.5 collective-permute-done.7
  (320 shorter events, 74.0 us)
Async XLA Ops:
  7.2 2.2 %copy-start = (f32[2,5,1,16384]{3,2,1,0:T(1,128)S(1)}, f32[2,5,1,16384]{3,2,1,0:T(1,128)}, u32[]{:S(2)}) copy-start(f32[2,5,1,16384]{3,2,1,0:T(1,128)} %param.11) | copy-start | bytes 1966084
  7.2 88.7 %all-reduce.4.cloned.1.call-start = ((), (), s32[]{:S(2)}) async-start(), calls=%async_computation | async-start | bytes 262144 | tf_op jit(solution)/shard_map/psum | solution.py:123
  48.4 0.7 copy-start.1
  99.0 1.6 copy-start.2
  99.0 10.4 %collective-permute-start.3 = (f32[128,256]{0,1:T(8,128)S(1)}, f32[128,256]{0,1:T(8,128)S(1)}, u32[]{:S(2)}, u32[]{:S(2)}) collective-permute-start(f32[128,256]{0,1:T(8,128)S(1)} %pad_maximum_fusion.4), channel_id=1, source_target_pairs={{252,0},{0,4},{4,8},{8,12},{12,16},{16,20},{20,24},{24,28},{28,32}... | collective-permute-start | bytes 393224 | tf_op jit(solution)/shard_map/ppermute | solution.py:20
  102.8 9.0 %collective-permute-start = (f32[128,256]{0,1:T(8,128)S(1)}, f32[128,256]{0,1:T(8,128)S(1)}, u32[]{:S(2)}, u32[]{:S(2)}) collective-permute-start(f32[128,256]{0,1:T(8,128)S(1)} %pad_maximum_fusion.3), channel_id=1, source_target_pairs={{4,0},{8,4},{12,8},{16,12},{20,16},{24,20},{28,24},{32,28},{36,32}... | collective-permute-start | bytes 393224 | tf_op jit(solution)/shard_map/ppermute | solution.py:20
  109.4 9.5 %collective-permute-start.4 = (f32[128,256]{0,1:T(8,128)S(1)}, f32[128,256]{0,1:T(8,128)S(1)}, u32[]{:S(2)}, u32[]{:S(2)}) collective-permute-start(f32[128,256]{0,1:T(8,128)S(1)} %collective-permute-done.3), channel_id=1, source_target_pairs={{252,0},{0,4},{4,8},{8,12},{12,16},{16,20},{20,24},{24,28},{28,32}... | collective-permute-start | bytes 393224 | tf_op jit(solution)/shard_map/ppermute | solution.py:20
  111.8 9.2 %collective-permute-start.1 = (f32[128,256]{0,1:T(8,128)S(1)}, f32[128,256]{0,1:T(8,128)S(1)}, u32[]{:S(2)}, u32[]{:S(2)}) collective-permute-start(f32[128,256]{0,1:T(8,128)S(1)} %collective-permute-done), channel_id=1, source_target_pairs={{4,0},{8,4},{12,8},{16,12},{20,16},{24,20},{28,24},{32,28},{36,32}... | collective-permute-start | bytes 393224 | tf_op jit(solution)/shard_map/ppermute | solution.py:20
  118.8 9.2 %collective-permute-start.5 = (f32[128,256]{0,1:T(8,128)S(1)}, f32[128,256]{0,1:T(8,128)S(1)}, u32[]{:S(2)}, u32[]{:S(2)}) collective-permute-start(f32[128,256]{0,1:T(8,128)S(1)} %collective-permute-done.4), channel_id=1, source_target_pairs={{252,0},{0,4},{4,8},{8,12},{12,16},{16,20},{20,24},{24,28},{28,32}... | collective-permute-start | bytes 393224 | tf_op jit(solution)/shard_map/ppermute | solution.py:20
  121.0 23.6 %collective-permute-start.2 = (f32[128,256]{0,1:T(8,128)S(1)}, f32[128,256]{0,1:T(8,128)S(1)}, u32[]{:S(2)}, u32[]{:S(2)}) collective-permute-start(f32[128,256]{0,1:T(8,128)S(1)} %collective-permute-done.1), channel_id=1, source_target_pairs={{4,0},{8,4},{12,8},{16,12},{20,16},{24,20},{28,24},{32,28},{36,32}... | collective-permute-start | bytes 393224 | tf_op jit(solution)/shard_map/ppermute | solution.py:20
  165.9 12.5 %collective-permute-start.6 = (f32[2,5,4096]{2,1,0:T(8,128)S(1)}, f32[2,5,4096]{2,1,0:T(8,128)S(1)}, u32[]{:S(2)}, u32[]{:S(2)}) collective-permute-start(f32[2,5,4096]{2,1,0:T(8,128)S(1)} %broadcast_select_fusion.1), channel_id=1, source_target_pairs={{0,4},{4,8},{8,12},{12,16},{16,20},{20,24},{24,28},{28,32},{32,36}... | collective-permute-start | bytes 491528 | tf_op jit(solution)/shard_map/ppermute | solution.py:26
  167.8 12.0 %collective-permute-start.7 = (f32[2,5,4096]{2,1,0:T(8,128)S(1)}, f32[2,5,4096]{2,1,0:T(8,128)S(1)}, u32[]{:S(2)}, u32[]{:S(2)}) collective-permute-start(f32[2,5,4096]{2,1,0:T(8,128)S(1)} %get-tuple-element.389), channel_id=1, source_target_pairs={{4,0},{8,4},{12,8},{16,12},{20,16},{24,20},{28,24},{32,28},{36,32}... | collective-permute-start | bytes 491528 | tf_op jit(solution)/shard_map/ppermute | solution.py:26
Sparse Core Ops, SparseCore 0:
  48.5 47.2 all-reduce.3
where the time goes:
time: 188 us
  matrix products  59.8 us (32%)
  waiting for transfers between devices  54.2 us (29%)
  starting transfers between devices  30.7 us (16%)
  local copies, waits for them, and re-layouts  16.4 us (9%)
  between operations  14.5 us (8%)
  other arithmetic  9.08 us (5%)
  loops' own time  3.06 us (2%)
    psum x1, waiting for transfers between devices, local(): density = lax.psum(partial_value, 'dom')  46.5 us
    dot_general x32, matrix products, accumulate(): lax.dot_general(onehot_rows, weighted_cols, (((0,), (0,)), ((), ())), pre...  35.1 us
    ppermute x6, starting transfers between devices, from_behind(): return lax.ppermute(block, axis, route)  20.6 us
    dot_general x32, matrix products, one_block(): jnp.dot(onehot_rows, field, precision=lax.Precision.HIGHEST, preferred_el...  19.6 us
    ppermute x2, starting transfers between devices, from_behind_2(): lax.ppermute(value, axis, [(source, source + steps) for source in range(f...  10.1 us
    dynamic_update_slice x64, local copies, waits for them, and re-layouts, lookup(): lax.map(one_block, (row_index.reshape(blocks, block_size), col_index.resh...  7.04 us
    ppermute x6, waiting for transfers between devices, from_behind(): return lax.ppermute(block, axis, route)  5.81 us
  transfers between devices with their start and end apart: 9, of which 8 were waited for; matrix products, arithmetic and copies ran while one was open for 11% of the time, Pallas kernels for 0%

commit v1 on v0

v1 whole, which is shorter than its diff:
```python
import functools
import math

import jax
import jax.numpy as jnp
import numpy as np
from jax import lax
from jax.experimental import pallas as pl
from jax.experimental.pallas import tpu as pltpu
from jax.sharding import PartitionSpec as P

MESH = pl.DeviceIdType.MESH
GRID = 128
SECTIONS = 3
ROWS = 128
BLOCK = 32
KICK_SCALE = 0.01
COS_X, SIN_X = (math.cos(2 * math.pi * 0.31), math.sin(2 * math.pi * 0.31))
COS_Y, SIN_Y = (math.cos(2 * math.pi * 0.32), math.sin(2 * math.pi * 0.32))
F32, BF16 = jnp.float32, jnp.bfloat16
PEERS = ((0, 1), (1, 0), (1, 1))


def constants():
    index = np.arange(1, GRID + 1)
    angle = (index[:, None] * index[None, :] % (2 * (GRID + 1))) * (np.pi / (GRID + 1))
    basis = math.sqrt(2.0 / (GRID + 1)) * np.sin(angle)
    padded = np.pad(basis, ((1, 1), (0, 0)))
    slope = (padded[:-2] - padded[2:]) * (0.5 * KICK_SCALE)
    eigen = 2.0 - 2.0 * np.cos(index * (np.pi / (GRID + 1)))
    inverse = 1.0 / (eigen[:, None] + eigen[None, :])
    return np.stack([basis, slope, inverse, slope.T]).astype(np.float32)


def dot(a, b):
    return jnp.dot(a, b, precision=lax.Precision.HIGHEST, preferred_element_type=F32)


def across(row):
    return jnp.broadcast_to(row, (GRID, 128))


def deposit(cells, weights, levels):
    row = (cells >> 7).astype(F32).astype(BF16)
    column = (cells & 127).astype(F32).astype(BF16)
    high = weights.astype(BF16)
    low = (weights - high.astype(F32)).astype(BF16)
    zero, one = jnp.zeros((GRID, 128), BF16), jnp.ones((GRID, 128), BF16)
    hit_column, part_high, part_low = [], [], []
    for i in range(cells.shape[0]):
        here = levels == across(row[i : i + 1])
        part_high.append(jnp.where(here, across(high[i : i + 1]), zero))
        part_low.append(jnp.where(here, across(low[i : i + 1]), zero))
        hit_column.append(jnp.where(levels == across(column[i : i + 1]), one, zero))
    left = jnp.concatenate(
        [jnp.concatenate(part_high, axis=1), jnp.concatenate(part_low, axis=1)], axis=0
    )
    right = jnp.concatenate(hit_column, axis=1)
    both = lax.dot_general(left, right, (((1,), (1,)), ((), ())), preferred_element_type=F32)
    return both[:GRID] + both[GRID:]


def lookup(cells, field, levels, row_levels):
    row = cells >> 7
    column = (cells & 127).astype(F32).astype(BF16)
    zero, one = jnp.zeros((GRID, 128), BF16), jnp.ones((GRID, 128), BF16)
    hit = jnp.concatenate(
        [jnp.where(levels == across(column[i : i + 1]), one, zero) for i in range(cells.shape[0])],
        axis=1,
    )
    picked = jnp.dot(field, jnp.concatenate([hit, hit], axis=0), preferred_element_type=F32)
    value_x, value_y = [], []
    for i in range(cells.shape[0]):
        here = row_levels == across(row[i : i + 1])
        lanes = slice(128 * i, 128 * (i + 1))
        value_x.append(jnp.sum(jnp.where(here, picked[:GRID, lanes], 0.0), axis=0, keepdims=True))
        value_y.append(jnp.sum(jnp.where(here, picked[GRID:, lanes], 0.0), axis=0, keepdims=True))
    return jnp.concatenate(value_x, axis=0), jnp.concatenate(value_y, axis=0)


def reversed_block(block):
    lanes = 127 - lax.broadcasted_iota(jnp.int32, (8, 128), 1)
    rows = 7 - lax.broadcasted_iota(jnp.int32, (8, 128), 0)
    pieces = []
    for i in reversed(range(block.shape[0] // 8)):
        piece = jnp.take_along_axis(block[8 * i : 8 * i + 8], lanes, axis=1)
        pieces.append(jnp.take_along_axis(piece, rows, axis=0))
    return jnp.concatenate(pieces, axis=0)


def turn(state):
    pos_x, mom_x, pos_y, mom_y = state
    return (
        COS_X * pos_x + SIN_X * mom_x,
        -SIN_X * pos_x + COS_X * mom_x,
        COS_Y * pos_y + SIN_Y * mom_y,
        -SIN_Y * pos_y + COS_Y * mom_y,
    )


def kicked(base, kick_x, kick_y):
    return (
        base[0] + SIN_X * kick_x,
        base[1] + COS_X * kick_x,
        base[2] + SIN_Y * kick_y,
        base[3] + COS_Y * kick_y,
    )


def kernel(
    slices,
    particles,
    cells,
    counts,
    table,
    kept,
    arrivals,
    state,
    cell,
    const,
    grid,
    pair_in,
    half,
    window_in,
    spectrum,
    field,
    out_state,
    leavers,
    leaver_kicks,
    arrived,
    arrived_kicks,
    in_sem,
    out_sem,
    pair_sem,
    window_sem,
    quarter_sem,
    leave_sem,
    kick_sem,
):
    me = lax.axis_index("cuts")
    dom = lax.axis_index("dom")
    y_hi, core = dom // 2, dom % 2

    def behind(distance):
        return lax.rem(me + (distance + slices), slices)

    def member(y_flip, core_flip):
        y = 1 - y_hi if y_flip else y_hi
        c = 1 - core if core_flip else core
        return y * 2 + c

    def send(src, dst, sems, index, cut, member_no):
        copy = pltpu.make_async_remote_copy(
            src_ref=src,
            dst_ref=dst,
            send_sem=sems.at[(0, *index)],
            recv_sem=sems.at[(1, *index)],
            device_id=(cut, member_no),
            device_id_type=MESH,
        )
        copy.start()
        return copy

    loads = {}
    for beam in (1, 0):
        loads["cells", beam] = pltpu.make_async_copy(
            cells.at[beam], cell.at[beam], in_sem.at[beam]
        )
        loads["weights", beam] = pltpu.make_async_copy(
            particles.at[beam, 4], state.at[beam, 4], in_sem.at[2 + beam]
        )
    for beam in (0, 1):
        loads["coords", beam] = pltpu.make_async_copy(
            particles.at[beam, pl.ds(0, 4)], state.at[beam, pl.ds(0, 4)], in_sem.at[4 + beam]
        )
    loads["table"] = pltpu.make_async_copy(table, const, in_sem.at[6])
    for load in loads.values():
        load.start()

    barrier = pltpu.get_barrier_semaphore()
    partners = [(me, member(*flips)) for flips in PEERS]
    for distance in range(1, SECTIONS + 1):
        for sign in (1, -1):
            for y_flip in (0, 1):
                partners.append((behind(sign * distance), member(y_flip, 0)))
    for partner in partners:
        pl.semaphore_signal(barrier, inc=1, device_id=partner, device_id_type=MESH)

    levels = lax.broadcasted_iota(jnp.int32, (GRID, 128), 0).astype(F32).astype(BF16)
    row_levels = lax.broadcasted_iota(jnp.int32, (GRID, 128), 0)
    copies = []

    def deposit_rows(beam, first, count, step):
        def some(i, total):
            rows = pl.ds(pl.multiple_of(first + i * step, step), step)
            return total + deposit(cell[beam, rows, :], state[beam, 4, rows, :], levels)

        return lax.fori_loop(0, count // step, some, jnp.zeros((GRID, GRID), F32))

    def pair_send(beam):
        other = pl.ds(pl.multiple_of((1 - core) * 64, 64), 64)
        copy = send(grid.at[beam, other], pair_in.at[beam], pair_sem, (beam,), me, member(0, 1))
        copies.append(copy)
        return copy

    def window_send(beam, pair_copy):
        pair_copy.wait_recv()
        mine = pl.ds(pl.multiple_of(core * 64, 64), 64)
        half[beam] = grid[beam, mine, :] + pair_in[beam]
        sent = []
        for distance in (1, 3, 2):
            for y_flip in (1, 0):
                y = 1 - y_hi if y_flip else y_hi
                rows = pl.ds(pl.multiple_of(y * BLOCK, BLOCK), BLOCK)
                cut = behind(-distance if beam == 1 else distance)
                sent.append(
                    send(
                        half.at[beam, rows],
                        window_in.at[beam, distance - 1, y_flip],
                        window_sem,
                        (beam, distance - 1, y_flip),
                        cut,
                        member(y_flip, 0),
                    )
                )
        copies.extend(sent)
        return sent

    def quarter_send(beam, window_copies):
        for copy in window_copies:
            copy.wait_recv()
        quarter = window_in[beam, 0, 0]
        for distance in range(SECTIONS):
            for y_flip in (0, 1):
                if distance or y_flip:
                    quarter = quarter + window_in[beam, distance, y_flip]
        rows = pl.ds(pl.multiple_of(core * 64 + y_hi * BLOCK, BLOCK), BLOCK)
        spectrum[beam, rows, :] = dot(quarter, const[0])
        sent = []
        for number, flips in enumerate(PEERS):
            place = spectrum.at[beam, rows]
            sent.append(send(place, place, quarter_sem, (beam, number), me, member(*flips)))
        copies.extend(sent)
        return sent

    def solve(beam, quarter_copies):
        for copy in quarter_copies:
            copy.wait_recv()
        basis, slope, inverse, slope_t = const[0], const[1], const[2], const[3]
        scaled = dot(basis, spectrum[beam]) * inverse
        both = dot(jnp.concatenate([slope, basis], axis=0), scaled)
        field_x = dot(both[:GRID], basis)
        field_y = dot(both[GRID:], slope_t)
        fields = jnp.concatenate([field_x, field_y], axis=0)
        high = fields.astype(BF16)
        low = (fields - high.astype(F32)).astype(BF16)
        field[beam] = jnp.concatenate([high, low], axis=1)

    row_place = lax.broadcasted_iota(jnp.int32, (BLOCK, 128), 0) * 128 + lax.broadcasted_iota(
        jnp.int32, (BLOCK, 128), 1
    )
    up_count = [jnp.where(me == slices - 1, 0, counts[beam, 0, 0, 0]) for beam in range(2)]
    down_count = [jnp.where(me == 0, 0, counts[beam, 1, 0, 0]) for beam in range(2)]

    def leave_send(beam):
        loads["coords", beam].wait()
        for way in range(2):
            rows = slice(ROWS - BLOCK, ROWS) if way == 0 else slice(0, BLOCK)
            limit = (up_count if way == 0 else down_count)[beam]
            base = turn([state[beam, comp, rows, :] for comp in range(4)])
            for comp, value in enumerate((*base, state[beam, 4, rows, :])):
                if way == 0:
                    value = reversed_block(value)
                leavers[way, beam, comp] = jnp.where(row_place < limit, value, 0.0)
            copies.append(
                send(
                    leavers.at[way, beam],
                    arrived.at[beam, :, pl.ds(way * BLOCK, BLOCK)],
                    leave_sem,
                    (way, beam),
                    behind(1 if way == 0 else -1),
                    dom,
                )
            )
        return copies[-2:]

    def look_up_block(beam, block):
        rows = pl.ds(pl.multiple_of(block * BLOCK, BLOCK), BLOCK)
        kick_x, kick_y = lookup(cell[beam, rows, :], field[1 - beam], levels, row_levels)
        place = row_place + block * (BLOCK * 128)
        stays = (place < ROWS * 128 - counts[beam, 0, 0, 0]) & (place >= counts[beam, 1, 0, 0])
        base = turn([state[beam, comp, rows, :] for comp in range(4)])
        for comp, value in enumerate(
            (*kicked(base, kick_x, kick_y), state[beam, 4, rows, :])
        ):
            out_state[beam, comp, rows, :] = jnp.where(stays, value, 0.0)
        return kick_x, kick_y

    def look_up(beam):
        sent = []
        def end(i, _):
            kick_x, kick_y = look_up_block(beam, i * 3)
            rows = pl.ds(pl.multiple_of(i * BLOCK, BLOCK), BLOCK)
            leaver_kicks[beam, 0, rows, :] = kick_x
            leaver_kicks[beam, 1, rows, :] = kick_y
            return 0

        lax.fori_loop(0, 2, end, 0)
        for comp in range(2):
            up = reversed_block(leaver_kicks[beam, comp, BLOCK:, :])
            leaver_kicks[beam, comp, BLOCK:, :] = jnp.where(row_place < up_count[beam], up, 0.0)
            down = leaver_kicks[beam, comp, :BLOCK, :]
            leaver_kicks[beam, comp, :BLOCK, :] = jnp.where(row_place < down_count[beam], down, 0.0)
        for way in range(2):
            sent.append(
                send(
                    leaver_kicks.at[beam, :, pl.ds((1 - way) * BLOCK, BLOCK)],
                    arrived_kicks.at[beam, :, pl.ds(way * BLOCK, BLOCK)],
                    kick_sem,
                    (way, beam),
                    behind(1 if way == 0 else -1),
                    dom,
                )
            )
        copies.extend(sent)

        def middle(i, _):
            look_up_block(beam, i + 1)
            return 0

        lax.fori_loop(0, 2, middle, 0)
        store = pltpu.make_async_copy(out_state.at[beam], kept.at[beam], out_sem.at[beam])
        store.start()
        return sent, store

    def arrive(beam, leave_copies, kick_copies):
        for copy in (*leave_copies, *kick_copies):
            copy.wait_recv()
        base = [arrived[beam, comp] for comp in range(4)]
        done = kicked(base, arrived_kicks[beam, 0], arrived_kicks[beam, 1])
        for comp in range(4):
            arrived[beam, comp] = done[comp]
        store = pltpu.make_async_copy(arrived.at[beam], arrivals.at[beam], out_sem.at[2 + beam])
        store.start()
        return store

    loads["cells", 1].wait()
    loads["weights", 1].wait()
    grid[1] = deposit_rows(1, 0, ROWS, 32)
    pl.semaphore_wait(barrier, len(partners))
    pair_1 = pair_send(1)
    loads["cells", 0].wait()
    loads["weights", 0].wait()
    first = deposit_rows(0, 0, ROWS // 2, 32)
    window_1 = window_send(1, pair_1)
    grid[0] = first + deposit_rows(0, ROWS // 2, ROWS // 2, 32)
    pair_0 = pair_send(0)
    loads["table"].wait()
    window_0 = window_send(0, pair_0)
    quarter_1 = quarter_send(1, window_1)
    leave_0 = leave_send(0)
    leave_1 = leave_send(1)
    quarter_0 = quarter_send(0, window_0)
    solve(1, quarter_1)
    kicks_0, store_0 = look_up(0)
    solve(0, quarter_0)
    kicks_1, store_1 = look_up(1)
    stores = [store_0, store_1]
    stores.append(arrive(0, leave_0, kicks_0))
    stores.append(arrive(1, leave_1, kicks_1))
    for copy in copies:
        copy.wait_send()
    for store in stores:
        store.wait()


def local(slices, particles, cells, counts):
    anywhere = pl.BlockSpec(memory_space=pl.ANY)
    dma = pltpu.SemaphoreType.DMA
    kept, arrivals = pl.pallas_call(
        functools.partial(kernel, slices),
        out_shape=(
            jax.ShapeDtypeStruct((2, 5, ROWS, 128), F32),
            jax.ShapeDtypeStruct((2, 5, 2 * BLOCK, 128), F32),
        ),
        in_specs=[
            anywhere,
            anywhere,
            pl.BlockSpec(memory_space=pltpu.SMEM),
            anywhere,
        ],
        out_specs=(anywhere, anywhere),
        scratch_shapes=[
            pltpu.VMEM((2, 5, ROWS, 128), F32),
            pltpu.VMEM((2, ROWS, 128), jnp.int32),
            pltpu.VMEM((4, GRID, GRID), F32),
            pltpu.VMEM((2, GRID, GRID), F32),
            pltpu.VMEM((2, GRID // 2, GRID), F32),
            pltpu.VMEM((2, GRID // 2, GRID), F32),
            pltpu.VMEM((2, SECTIONS, 2, BLOCK, GRID), F32),
            pltpu.VMEM((2, GRID, GRID), F32),
            pltpu.VMEM((2, 2 * GRID, 2 * GRID), BF16),
            pltpu.VMEM((2, 5, ROWS, 128), F32),
            pltpu.VMEM((2, 2, 5, BLOCK, 128), F32),
            pltpu.VMEM((2, 2, 2 * BLOCK, 128), F32),
            pltpu.VMEM((2, 5, 2 * BLOCK, 128), F32),
            pltpu.VMEM((2, 2, 2 * BLOCK, 128), F32),
            dma((7,)),
            dma((4,)),
            dma((2, 2)),
            dma((2, 2, SECTIONS, 2)),
            dma((2, 2, 3)),
            dma((2, 2, 2)),
            dma((2, 2, 2)),
        ],
        compiler_params=pltpu.CompilerParams(
            collective_id=0, has_side_effects=True, vmem_limit_bytes=56 * 2**20
        ),
        cost_estimate=pl.CostEstimate(
            flops=7 * 10**9, bytes_accessed=2 * 10**6, transcendentals=0
        ),
        name="crossing",
    )(
        particles.reshape(2, 5, ROWS, 128),
        cells.reshape(2, ROWS, 128),
        counts,
        jnp.asarray(constants()),
    )
    return kept.reshape(2, 5, 1, ROWS * 128), arrivals.reshape(2, 5, 1, 2 * BLOCK * 128)


def solution(mesh):
    return jax.shard_map(
        functools.partial(local, mesh.shape["cuts"]),
        mesh=mesh,
        in_specs=(
            P(None, None, "cuts", "dom"),
            P(None, "cuts", "dom"),
            P(None, None, "cuts", "dom"),
        ),
        out_specs=(P(None, None, "cuts", "dom"), P(None, None, "cuts", "dom")),
        check_vma=False,
    )
```

time: 188 us -> 42.9 us (0.23)
  the two profiles are of different devices: /device:TPU:8 before, /device:TPU:1 now
where the time goes in v1:
time: 42.9 us; the launch traced here: 42.7 us
  Pallas kernels  38 us (89%)
  local copies, waits for them, and re-layouts  4.09 us (10%)
  between operations  0.66 us (2%)
    pallas_call x1, Pallas kernels, local(): pl.pallas_call(functools.partial(kernel, slices), out_shape=(jax.ShapeDty...  38 us
    unnamed x7, local copies, waits for them, and re-layouts  4.09 us

profile of v1, /device:TPU:1, one launch (start us, length us, event | category | flops | bytes accessed | tf_op | source)
XLA Modules:
  0.0 42.7 jit_solution(11438280206725703456)
XLA Ops:
  0.6 0.0 copy-start.1
  0.6 0.7 %copy-done.1 = s32[2,2,1,1]{1,3,2,0:T(1,128)S(1)} copy-done((s32[2,2,1,1]{1,3,2,0:T(1,128)S(1)}, s32[2,2,1,1]{1,3,2,0:T(1,128)}, u32[]{:S(2)}) %copy-start.1) | copy-done | bytes 40
  1.3 0.7 %copy.9.counts = s32[2,2,1,1]{3,2,1,0:T(1,128)} copy(s32[2,2,1,1]{1,3,2,0:T(1,128)S(1)} %copy-done.1) | data formatting | bytes 32 | tf_op args[2]
  2.0 38.0 %crossing.1 = (f32[2,5,128,128]{3,2,1,0:T(8,128)}, f32[2,5,64,128]{3,2,1,0:T(8,128)}) custom-call(f32[2,5,128,128]{3,2,1,0:T(8,128)} %bitcast.6, s32[2,128,128]{2,1,0:T(8,128)} %bitcast.7, s32[2,2,1,1]{3,2,1,0:T(1,128)} %copy.9.counts, f32[4,128,128]{2,1,0:T(8,128)} %constant.2.clone.table), custom_call_target="tpu_custom_call" | custom-call | flops 7000000000 | bytes 2000000 | tf_op jit(solution)/shard_map/crossing/pallas_call | solution.py:380
  40.0 0.0 copy-start
  40.0 2.0 %copy.20 = f32[2,5,1,16384]{3,2,1,0:T(1,128)} copy(f32[2,5,1,16384]{3,2,1,0:T(1,128)} %bitcast.4) | data formatting | bytes 1310720
  42.0 0.0 copy-done
  42.0 0.7 %copy.21 = f32[2,5,1,8192]{3,2,1,0:T(1,128)} copy(f32[2,5,1,8192]{3,2,1,0:T(1,128)S(1)} %bitcast.5) | data formatting | bytes 655360
Async XLA Ops:
  0.6 0.7 %copy-start.1 = (s32[2,2,1,1]{1,3,2,0:T(1,128)S(1)}, s32[2,2,1,1]{1,3,2,0:T(1,128)}, u32[]{:S(2)}) copy-start(s32[2,2,1,1]{1,3,2,0:T(1,128)} %param.6) | copy-start | bytes 52
  40.0 2.0 %copy-start = (f32[2,5,64,128]{3,2,1,0:T(8,128)S(1)}, f32[2,5,64,128]{3,2,1,0:T(8,128)}, u32[]{:S(2)}) copy-start(f32[2,5,64,128]{3,2,1,0:T(8,128)} %get-tuple-element.5) | copy-start | bytes 983044

commit v2 on v1

--- a/solution.py
+++ b/solution.py
@@ -18,7 +18,6 @@
 COS_X, SIN_X = (math.cos(2 * math.pi * 0.31), math.sin(2 * math.pi * 0.31))
 COS_Y, SIN_Y = (math.cos(2 * math.pi * 0.32), math.sin(2 * math.pi * 0.32))
 F32, BF16 = jnp.float32, jnp.bfloat16
-PEERS = ((0, 1), (1, 0), (1, 1))
 
 
 def constants():
@@ -111,29 +110,28 @@
     slices,
     particles,
     cells,
-    counts,
+    counts_in,
     table,
     kept,
     arrivals,
     state,
     cell,
     const,
+    counts,
     grid,
     pair_in,
     half,
     window_in,
     spectrum,
     field,
-    out_state,
     leavers,
     leaver_kicks,
     arrived,
     arrived_kicks,
     in_sem,
-    out_sem,
     pair_sem,
     window_sem,
-    quarter_sem,
+    share_sem,
     leave_sem,
     kick_sem,
 ):
@@ -162,7 +160,7 @@
         return copy
 
     loads = {}
-    for beam in (1, 0):
+    for beam in (0, 1):
         loads["cells", beam] = pltpu.make_async_copy(
             cells.at[beam], cell.at[beam], in_sem.at[beam]
         )
@@ -174,11 +172,12 @@
             particles.at[beam, pl.ds(0, 4)], state.at[beam, pl.ds(0, 4)], in_sem.at[4 + beam]
         )
     loads["table"] = pltpu.make_async_copy(table, const, in_sem.at[6])
+    loads["counts"] = pltpu.make_async_copy(counts_in, counts, in_sem.at[7])
     for load in loads.values():
         load.start()
 
     barrier = pltpu.get_barrier_semaphore()
-    partners = [(me, member(*flips)) for flips in PEERS]
+    partners = [(me, member(0, 1))]
     for distance in range(1, SECTIONS + 1):
         for sign in (1, -1):
             for y_flip in (0, 1):
@@ -208,14 +207,12 @@
         mine = pl.ds(pl.multiple_of(core * 64, 64), 64)
         half[beam] = grid[beam, mine, :] + pair_in[beam]
         sent = []
-        for distance in (1, 3, 2):
+        for distance in (2, 3, 1):
             for y_flip in (1, 0):
-                y = 1 - y_hi if y_flip else y_hi
-                rows = pl.ds(pl.multiple_of(y * BLOCK, BLOCK), BLOCK)
                 cut = behind(-distance if beam == 1 else distance)
                 sent.append(
                     send(
-                        half.at[beam, rows],
+                        half.at[beam],
                         window_in.at[beam, distance - 1, y_flip],
                         window_sem,
                         (beam, distance - 1, y_flip),
@@ -226,26 +223,23 @@
         copies.extend(sent)
         return sent
 
-    def quarter_send(beam, window_copies):
+    def share(beam, window_copies):
         for copy in window_copies:
             copy.wait_recv()
-        quarter = window_in[beam, 0, 0]
+        total = window_in[beam, 0, 0]
         for distance in range(SECTIONS):
             for y_flip in (0, 1):
                 if distance or y_flip:
-                    quarter = quarter + window_in[beam, distance, y_flip]
-        rows = pl.ds(pl.multiple_of(core * 64 + y_hi * BLOCK, BLOCK), BLOCK)
-        spectrum[beam, rows, :] = dot(quarter, const[0])
-        sent = []
-        for number, flips in enumerate(PEERS):
-            place = spectrum.at[beam, rows]
-            sent.append(send(place, place, quarter_sem, (beam, number), me, member(*flips)))
-        copies.extend(sent)
-        return sent
-
-    def solve(beam, quarter_copies):
-        for copy in quarter_copies:
-            copy.wait_recv()
+                    total = total + window_in[beam, distance, y_flip]
+        rows = pl.ds(pl.multiple_of(core * 64, 64), 64)
+        spectrum[beam, rows, :] = dot(total, const[0])
+        place = spectrum.at[beam, rows]
+        copy = send(place, place, share_sem, (beam,), me, member(0, 1))
+        copies.append(copy)
+        return copy
+
+    def solve(beam, share_copy):
+        share_copy.wait_recv()
         basis, slope, inverse, slope_t = const[0], const[1], const[2], const[3]
         scaled = dot(basis, spectrum[beam]) * inverse
         both = dot(jnp.concatenate([slope, basis], axis=0), scaled)
@@ -259,10 +253,7 @@
     row_place = lax.broadcasted_iota(jnp.int32, (BLOCK, 128), 0) * 128 + lax.broadcasted_iota(
         jnp.int32, (BLOCK, 128), 1
     )
-    up_count = [jnp.where(me == slices - 1, 0, counts[beam, 0, 0, 0]) for beam in range(2)]
-    down_count = [jnp.where(me == 0, 0, counts[beam, 1, 0, 0]) for beam in range(2)]
-
-    def leave_send(beam):
+    def leave_pack(beam):
         loads["coords", beam].wait()
         for way in range(2):
             rows = slice(ROWS - BLOCK, ROWS) if way == 0 else slice(0, BLOCK)
@@ -272,6 +263,9 @@
                 if way == 0:
                     value = reversed_block(value)
                 leavers[way, beam, comp] = jnp.where(row_place < limit, value, 0.0)
+
+    def leave_send(beam):
+        for way in range(2):
             copies.append(
                 send(
                     leavers.at[way, beam],
@@ -288,144 +282,155 @@
         rows = pl.ds(pl.multiple_of(block * BLOCK, BLOCK), BLOCK)
         kick_x, kick_y = lookup(cell[beam, rows, :], field[1 - beam], levels, row_levels)
         place = row_place + block * (BLOCK * 128)
-        stays = (place < ROWS * 128 - counts[beam, 0, 0, 0]) & (place >= counts[beam, 1, 0, 0])
+        stays = (place < ROWS * 128 - counts[beam, 0, 0, 0]) & (place >= counts[beam, 0, 0, 1])
         base = turn([state[beam, comp, rows, :] for comp in range(4)])
         for comp, value in enumerate(
             (*kicked(base, kick_x, kick_y), state[beam, 4, rows, :])
         ):
-            out_state[beam, comp, rows, :] = jnp.where(stays, value, 0.0)
+            kept[beam, comp, rows, :] = jnp.where(stays, value, 0.0)
         return kick_x, kick_y
 
-    def look_up(beam):
-        sent = []
-        def end(i, _):
-            kick_x, kick_y = look_up_block(beam, i * 3)
-            rows = pl.ds(pl.multiple_of(i * BLOCK, BLOCK), BLOCK)
-            leaver_kicks[beam, 0, rows, :] = kick_x
-            leaver_kicks[beam, 1, rows, :] = kick_y
-            return 0
-
-        lax.fori_loop(0, 2, end, 0)
-        for comp in range(2):
-            up = reversed_block(leaver_kicks[beam, comp, BLOCK:, :])
-            leaver_kicks[beam, comp, BLOCK:, :] = jnp.where(row_place < up_count[beam], up, 0.0)
-            down = leaver_kicks[beam, comp, :BLOCK, :]
-            leaver_kicks[beam, comp, :BLOCK, :] = jnp.where(row_place < down_count[beam], down, 0.0)
-        for way in range(2):
-            sent.append(
-                send(
-                    leaver_kicks.at[beam, :, pl.ds((1 - way) * BLOCK, BLOCK)],
-                    arrived_kicks.at[beam, :, pl.ds(way * BLOCK, BLOCK)],
-                    kick_sem,
-                    (way, beam),
-                    behind(1 if way == 0 else -1),
-                    dom,
-                )
-            )
-        copies.extend(sent)
-
+    def look_up_end(beam, end):
+        kick_x, kick_y = look_up_block(beam, end * 3)
+        rows = slice(end * BLOCK, (end + 1) * BLOCK)
+        limit = (down_count if end == 0 else up_count)[beam]
+        for comp, kick in enumerate((kick_x, kick_y)):
+            if end == 1:
+                kick = reversed_block(kick)
+            leaver_kicks[beam, comp, rows, :] = jnp.where(row_place < limit, kick, 0.0)
+        way = 1 - end
+        copy = send(
+            leaver_kicks.at[beam, :, pl.ds(end * BLOCK, BLOCK)],
+            arrived_kicks.at[beam, :, pl.ds(way * BLOCK, BLOCK)],
+            kick_sem,
+            (way, beam),
+            behind(1 if way == 0 else -1),
+            dom,
+        )
+        copies.append(copy)
+        return copy
+
+    def look_up_middle(beam):
         def middle(i, _):
             look_up_block(beam, i + 1)
             return 0
 
         lax.fori_loop(0, 2, middle, 0)
-        store = pltpu.make_async_copy(out_state.at[beam], kept.at[beam], out_sem.at[beam])
-        store.start()
-        return sent, store
 
     def arrive(beam, leave_copies, kick_copies):
         for copy in (*leave_copies, *kick_copies):
             copy.wait_recv()
         base = [arrived[beam, comp] for comp in range(4)]
         done = kicked(base, arrived_kicks[beam, 0], arrived_kicks[beam, 1])
-        for comp in range(4):
-            arrived[beam, comp] = done[comp]
-        store = pltpu.make_async_copy(arrived.at[beam], arrivals.at[beam], out_sem.at[2 + beam])
-        store.start()
-        return store
-
+        for comp, value in enumerate((*done, arrived[beam, 4])):
+            arrivals[beam, comp] = value
+
+    loads["cells", 0].wait()
+    loads["weights", 0].wait()
+    grid[0] = deposit_rows(0, 0, ROWS, ROWS)
+    pl.semaphore_wait(barrier, len(partners))
+    pair_0 = pair_send(0)
     loads["cells", 1].wait()
     loads["weights", 1].wait()
-    grid[1] = deposit_rows(1, 0, ROWS, 32)
-    pl.semaphore_wait(barrier, len(partners))
+    first = deposit_rows(1, 0, ROWS // 2, ROWS // 2)
+    window_0 = window_send(0, pair_0)
+    grid[1] = first + deposit_rows(1, ROWS // 2, ROWS // 2, ROWS // 2)
     pair_1 = pair_send(1)
-    loads["cells", 0].wait()
-    loads["weights", 0].wait()
-    first = deposit_rows(0, 0, ROWS // 2, 32)
+    loads["counts"].wait()
+    up_count = [jnp.where(me == slices - 1, 0, counts[beam, 0, 0, 0]) for beam in range(2)]
+    down_count = [jnp.where(me == 0, 0, counts[beam, 0, 0, 1]) for beam in range(2)]
+    for beam in range(2):
+        leave_pack(beam)
     window_1 = window_send(1, pair_1)
-    grid[0] = first + deposit_rows(0, ROWS // 2, ROWS // 2, 32)
-    pair_0 = pair_send(0)
+    leave = [leave_send(beam) for beam in range(2)]
     loads["table"].wait()
-    window_0 = window_send(0, pair_0)
-    quarter_1 = quarter_send(1, window_1)
-    leave_0 = leave_send(0)
-    leave_1 = leave_send(1)
-    quarter_0 = quarter_send(0, window_0)
-    solve(1, quarter_1)
-    kicks_0, store_0 = look_up(0)
-    solve(0, quarter_0)
-    kicks_1, store_1 = look_up(1)
-    stores = [store_0, store_1]
-    stores.append(arrive(0, leave_0, kicks_0))
-    stores.append(arrive(1, leave_1, kicks_1))
+    share_0 = share(0, window_0)
+    solve(0, share_0)
+    kicks_1 = [look_up_end(1, 0)]
+    share_1 = share(1, window_1)
+    kicks_1.append(look_up_end(1, 1))
+    solve(1, share_1)
+    kicks_0 = [look_up_end(0, 0), look_up_end(0, 1)]
+    look_up_middle(1)
+    look_up_middle(0)
+    arrive(1, leave[1], kicks_1)
+    arrive(0, leave[0], kicks_0)
     for copy in copies:
         copy.wait_send()
+
+
+def store_kernel(kept_in, arrivals_in, kept, arrivals, sems):
+    stores = [
+        pltpu.make_async_copy(kept_in, kept, sems.at[0]),
+        pltpu.make_async_copy(arrivals_in, arrivals, sems.at[1]),
+    ]
+    for store in stores:
+        store.start()
     for store in stores:
         store.wait()
 
 
 def local(slices, particles, cells, counts):
-    anywhere = pl.BlockSpec(memory_space=pl.ANY)
+    in_hbm = pl.BlockSpec(memory_space=pltpu.HBM)
     dma = pltpu.SemaphoreType.DMA
-    kept, arrivals = pl.pallas_call(
+    in_vmem = pl.BlockSpec(memory_space=pltpu.VMEM)
+    shapes = (
+        jax.ShapeDtypeStruct((2, 5, ROWS, 128), F32),
+        jax.ShapeDtypeStruct((2, 5, 2 * BLOCK, 128), F32),
+    )
+    results = pl.pallas_call(
         functools.partial(kernel, slices),
-        out_shape=(
-            jax.ShapeDtypeStruct((2, 5, ROWS, 128), F32),
-            jax.ShapeDtypeStruct((2, 5, 2 * BLOCK, 128), F32),
-        ),
+        out_shape=shapes,
         in_specs=[
-            anywhere,
-            anywhere,
-            pl.BlockSpec(memory_space=pltpu.SMEM),
-            anywhere,
+            in_hbm,
+            in_hbm,
+            in_hbm,
+            in_hbm,
         ],
-        out_specs=(anywhere, anywhere),
+        out_specs=(in_vmem, in_vmem),
         scratch_shapes=[
             pltpu.VMEM((2, 5, ROWS, 128), F32),
             pltpu.VMEM((2, ROWS, 128), jnp.int32),
             pltpu.VMEM((4, GRID, GRID), F32),
+            pltpu.SMEM((2, 1, 1, 2), jnp.int32),
             pltpu.VMEM((2, GRID, GRID), F32),
             pltpu.VMEM((2, GRID // 2, GRID), F32),
             pltpu.VMEM((2, GRID // 2, GRID), F32),
-            pltpu.VMEM((2, SECTIONS, 2, BLOCK, GRID), F32),
+            pltpu.VMEM((2, SECTIONS, 2, GRID // 2, GRID), F32),
             pltpu.VMEM((2, GRID, GRID), F32),
             pltpu.VMEM((2, 2 * GRID, 2 * GRID), BF16),
-            pltpu.VMEM((2, 5, ROWS, 128), F32),
             pltpu.VMEM((2, 2, 5, BLOCK, 128), F32),
             pltpu.VMEM((2, 2, 2 * BLOCK, 128), F32),
             pltpu.VMEM((2, 5, 2 * BLOCK, 128), F32),
             pltpu.VMEM((2, 2, 2 * BLOCK, 128), F32),
-            dma((7,)),
-            dma((4,)),
+            dma((8,)),
             dma((2, 2)),
             dma((2, 2, SECTIONS, 2)),
-            dma((2, 2, 3)),
+            dma((2, 2)),
             dma((2, 2, 2)),
             dma((2, 2, 2)),
         ],
         compiler_params=pltpu.CompilerParams(
-            collective_id=0, has_side_effects=True, vmem_limit_bytes=56 * 2**20
+            collective_id=0, has_side_effects=True, vmem_limit_bytes=40 * 2**20
         ),
         cost_estimate=pl.CostEstimate(
             flops=7 * 10**9, bytes_accessed=2 * 10**6, transcendentals=0
         ),
         name="crossing",
     )(
-        particles.reshape(2, 5, ROWS, 128),
-        cells.reshape(2, ROWS, 128),
-        counts,
-        jnp.asarray(constants()),
-    )
+        pltpu.with_memory_space_constraint(particles.reshape(2, 5, ROWS, 128), pltpu.HBM),
+        pltpu.with_memory_space_constraint(cells.reshape(2, ROWS, 128), pltpu.HBM),
+        pltpu.with_memory_space_constraint(counts.transpose(0, 2, 3, 1), pltpu.HBM),
+        pltpu.with_memory_space_constraint(jnp.asarray(constants()), pltpu.HBM),
+    )
+    kept, arrivals = pl.pallas_call(
+        store_kernel,
+        out_shape=shapes,
+        in_specs=[in_vmem, in_vmem],
+        out_specs=(in_hbm, in_hbm),
+        scratch_shapes=[dma((2,))],
+        name="store",
+    )(*results)
     return kept.reshape(2, 5, 1, ROWS * 128), arrivals.reshape(2, 5, 1, 2 * BLOCK * 128)
 
 

time: 42.9 us -> 40.1 us (0.935)
  local copies, waits for them, and re-layouts: 4.09 us -> 1.57 us
    unnamed x7 -> x4, local copies, waits for them, and re-layouts: 4.09 us -> 1.57 us
    pallas_call x1 -> x2, Pallas kernels: 38 us -> 37.8 us  [the longest x1 35.6 us: local(): pl.pallas_call(functools.partial(kernel, slices), out_shape=shapes, in_sp...]
where the time goes in v2:
time: 40.1 us; the launch traced here: 40 us
  Pallas kernels  37.8 us (94%)
  local copies, waits for them, and re-layouts  1.57 us (4%)
  between operations  0.65 us (2%)
    pallas_call x1, Pallas kernels, local(): pl.pallas_call(functools.partial(kernel, slices), out_shape=shapes, in_sp...  35.6 us
    pallas_call x1, Pallas kernels, local(): pl.pallas_call(store_kernel, out_shape=shapes, in_specs=[in_vmem, in_vmem...  2.12 us
    unnamed x4, local copies, waits for them, and re-layouts  1.57 us

profile of v2, /device:TPU:1, one launch (start us, length us, event | category | flops | bytes accessed | tf_op | source)
XLA Modules:
  0.0 40.0 jit_solution(8831133452205630875)
XLA Ops:
  0.6 35.6 %crossing.1 = (f32[2,5,128,128]{3,2,1,0:T(8,128)S(1)}, f32[2,5,64,128]{3,2,1,0:T(8,128)S(1)}) custom-call(f32[2,5,128,128]{3,2,1,0:T(8,128)} %bitcast.7, s32[2,128,128]{2,1,0:T(8,128)} %bitcast.10, s32[2,1,1,2]{3,2,1,0:T(1,128)} %bitcast.11, f32[4,128,128]{2,1,0:T(8,128)} %constant.2.clone.table), custom_call_target="tpu_custom_call" | custom-call | flops 7000000000 | bytes 2000000 | tf_op jit(solution)/shard_map/crossing/pallas_call | solution.py:381
  36.3 0.0 copy-start
  36.3 0.8 %copy-done = f32[2,5,128,128]{3,2,1,0:T(8,128)} copy-done((f32[2,5,128,128]{3,2,1,0:T(8,128)}, f32[2,5,128,128]{3,2,1,0:T(8,128)S(1)}, u32[]{:S(2)}) %copy-start) | copy-done | bytes 655384
  37.1 0.0 copy-start.1
  37.1 0.7 %copy-done.1 = f32[2,5,64,128]{3,2,1,0:T(8,128)} copy-done((f32[2,5,64,128]{3,2,1,0:T(8,128)}, f32[2,5,64,128]{3,2,1,0:T(8,128)S(1)}, u32[]{:S(2)}) %copy-start.1) | copy-done | bytes 327704
  37.9 2.1 %store.1 = (f32[2,5,128,128]{3,2,1,0:T(8,128)}, f32[2,5,64,128]{3,2,1,0:T(8,128)}) custom-call(f32[2,5,128,128]{3,2,1,0:T(8,128)} %copy-done, f32[2,5,64,128]{3,2,1,0:T(8,128)} %copy-done.1), custom_call_target="tpu_custom_call" | custom-call | tf_op jit(solution)/shard_map/store/pallas_call | solution.py:426
Async XLA Ops:
  36.3 0.8 %copy-start = (f32[2,5,128,128]{3,2,1,0:T(8,128)}, f32[2,5,128,128]{3,2,1,0:T(8,128)S(1)}, u32[]{:S(2)}) copy-start(f32[2,5,128,128]{3,2,1,0:T(8,128)S(1)} %get-tuple-element.6.kept_in) | copy-start | bytes 1966084
  37.1 0.7 %copy-start.1 = (f32[2,5,64,128]{3,2,1,0:T(8,128)}, f32[2,5,64,128]{3,2,1,0:T(8,128)S(1)}, u32[]{:S(2)}) copy-start(f32[2,5,64,128]{3,2,1,0:T(8,128)S(1)} %get-tuple-element.7.arrivals_in) | copy-start | bytes 983044

commit v3 on v2

v3 whole, which is shorter than its diff:
```python
import functools
import math

import jax
import jax.numpy as jnp
import numpy as np
from jax import lax
from jax.experimental import pallas as pl
from jax.experimental.pallas import tpu as pltpu
from jax.sharding import PartitionSpec as P

MESH = pl.DeviceIdType.MESH
GRID = 128
SECTIONS = 3
ROWS = 128
BLOCK = 32
DEPOSIT_ROWS = 64
LOOK_ROWS = 32
KICK_SCALE = 0.01
COS_X, SIN_X = (math.cos(2 * math.pi * 0.31), math.sin(2 * math.pi * 0.31))
COS_Y, SIN_Y = (math.cos(2 * math.pi * 0.32), math.sin(2 * math.pi * 0.32))
F32, BF16 = jnp.float32, jnp.bfloat16


def parts(values):
    high = values.astype(BF16)
    return high, (values - high.astype(F32)).astype(BF16)


def left_factor(a):
    high, low = parts(a)
    return jnp.concatenate([high, high, low], axis=1)


def right_factor(b):
    high, low = parts(b)
    return jnp.concatenate([high, low, high], axis=0)


def constants():
    index = np.arange(1, GRID + 1)
    angle = (index[:, None] * index[None, :] % (2 * (GRID + 1))) * (np.pi / (GRID + 1))
    basis = math.sqrt(2.0 / (GRID + 1)) * np.sin(angle)
    padded = np.pad(basis, ((1, 1), (0, 0)))
    slope = (padded[:-2] - padded[2:]) * (0.5 * KICK_SCALE)
    eigen = 2.0 - 2.0 * np.cos(index * (np.pi / (GRID + 1)))
    inverse = 1.0 / (eigen[:, None] + eigen[None, :])
    order = np.concatenate([np.arange(0, GRID, 2), np.arange(1, GRID, 2)])
    return np.stack([basis, slope[order], basis[order], slope.T, inverse]).astype(np.float32)


def times_const(a, right):
    return jnp.dot(left_factor(a), right, preferred_element_type=F32)


def const_times(left, b):
    return jnp.dot(left, right_factor(b), preferred_element_type=F32)


def across(row):
    return jnp.broadcast_to(row, (GRID, 128))


def deposit(cells, weights, levels):
    row = (cells >> 7).astype(F32).astype(BF16)
    column = (cells & 127).astype(F32).astype(BF16)
    high, low = parts(weights)
    zero, one = jnp.zeros((GRID, 128), BF16), jnp.ones((GRID, 128), BF16)
    hit_column, part_high, part_low = [], [], []
    for i in range(cells.shape[0]):
        here = levels == across(row[i : i + 1])
        part_high.append(jnp.where(here, across(high[i : i + 1]), zero))
        part_low.append(jnp.where(here, across(low[i : i + 1]), zero))
        hit_column.append(jnp.where(levels == across(column[i : i + 1]), one, zero))
    left = jnp.concatenate(
        [jnp.concatenate(part_high, axis=1), jnp.concatenate(part_low, axis=1)], axis=0
    )
    right = jnp.concatenate(hit_column, axis=1)
    both = lax.dot_general(left, right, (((1,), (1,)), ((), ())), preferred_element_type=F32)
    return both[:GRID] + both[GRID:]


def lookup(cells, field, levels, row_levels):
    pair = cells >> 8
    place = (cells & 255).astype(F32).astype(BF16)
    zero, one = jnp.zeros((2 * GRID, 128), BF16), jnp.ones((2 * GRID, 128), BF16)
    half = GRID // 2
    value_x, value_y = [], []
    for first in range(0, cells.shape[0], 2):
        hits = [
            jnp.where(levels == jnp.broadcast_to(place[i : i + 1], (2 * GRID, 128)), one, zero)
            for i in (first, first + 1)
        ]
        picked = jnp.dot(field, jnp.concatenate(hits, axis=1), preferred_element_type=F32)
        for i in (0, 1):
            here = row_levels == jnp.broadcast_to(pair[first + i : first + i + 1], (half, 128))
            part = picked[:, 128 * i : 128 * (i + 1)]
            both_x = part[:half] + part[GRID : GRID + half]
            both_y = part[half:GRID] + part[GRID + half :]
            value_x.append(jnp.sum(jnp.where(here, both_x, 0.0), axis=0, keepdims=True))
            value_y.append(jnp.sum(jnp.where(here, both_y, 0.0), axis=0, keepdims=True))
    return jnp.concatenate(value_x, axis=0), jnp.concatenate(value_y, axis=0)


def reversed_block(block):
    lanes = 127 - lax.broadcasted_iota(jnp.int32, (8, 128), 1)
    rows = 7 - lax.broadcasted_iota(jnp.int32, (8, 128), 0)
    pieces = []
    for i in reversed(range(block.shape[0] // 8)):
        piece = jnp.take_along_axis(block[8 * i : 8 * i + 8], lanes, axis=1)
        pieces.append(jnp.take_along_axis(piece, rows, axis=0))
    return jnp.concatenate(pieces, axis=0)


def turn(state):
    pos_x, mom_x, pos_y, mom_y = state
    return (
        COS_X * pos_x + SIN_X * mom_x,
        -SIN_X * pos_x + COS_X * mom_x,
        COS_Y * pos_y + SIN_Y * mom_y,
        -SIN_Y * pos_y + COS_Y * mom_y,
    )


def kicked(base, kick_x, kick_y):
    return (
        base[0] + SIN_X * kick_x,
        base[1] + COS_X * kick_x,
        base[2] + SIN_Y * kick_y,
        base[3] + COS_Y * kick_y,
    )


def kernel(
    slices,
    particles,
    cells,
    counts_in,
    table,
    kept,
    arrived,
    arrived_kicks,
    state,
    cell,
    const,
    lefts,
    rights,
    counts,
    grid,
    pair_in,
    half,
    window_in,
    spectrum,
    field,
    leavers,
    kicks,
    leaver_kicks,
    in_sem,
    pair_sem,
    window_sem,
    share_sem,
    leave_sem,
    kick_sem,
):
    me = lax.axis_index("cuts")
    dom = lax.axis_index("dom")
    y_hi, core = dom // 2, dom % 2

    def behind(distance):
        return lax.rem(me + (distance + slices), slices)

    def member(y_flip, core_flip):
        y = 1 - y_hi if y_flip else y_hi
        c = 1 - core if core_flip else core
        return y * 2 + c

    def remote(src, dst, sems, index, cut, member_no):
        copy = pltpu.make_async_remote_copy(
            src_ref=src,
            dst_ref=dst,
            send_sem=sems.at[(0, *index)],
            recv_sem=sems.at[(1, *index)],
            device_id=(cut, member_no),
            device_id_type=MESH,
        )
        return copy

    loads = {}
    for beam in (0, 1):
        loads["cells", beam] = pltpu.make_async_copy(
            cells.at[beam], cell.at[beam], in_sem.at[beam]
        )
        loads["weights", beam] = pltpu.make_async_copy(
            particles.at[beam, 4], state.at[beam, 4], in_sem.at[2 + beam]
        )
    for beam in (0, 1):
        loads["coords", beam] = pltpu.make_async_copy(
            particles.at[beam, pl.ds(0, 4)], state.at[beam, pl.ds(0, 4)], in_sem.at[4 + beam]
        )
    loads["table"] = pltpu.make_async_copy(table, const, in_sem.at[6])
    loads["counts"] = pltpu.make_async_copy(counts_in, counts, in_sem.at[7])
    for load in loads.values():
        load.start()

    barrier = pltpu.get_barrier_semaphore()
    partners = [(me, member(0, 1))]
    for distance in range(1, SECTIONS + 1):
        for sign in (1, -1):
            for y_flip in (0, 1):
                partners.append((behind(sign * distance), member(y_flip, 0)))
    for partner in partners:
        pl.semaphore_signal(barrier, inc=1, device_id=partner, device_id_type=MESH)

    pair_levels = lax.broadcasted_iota(jnp.int32, (2 * GRID, 128), 0).astype(F32).astype(BF16)
    levels = pair_levels[:GRID]
    row_levels = lax.broadcasted_iota(jnp.int32, (GRID // 2, 128), 0)
    def pair_copy(beam):
        other = pl.ds(pl.multiple_of((1 - core) * 64, 64), 64)
        return remote(grid.at[beam, other], pair_in.at[beam], pair_sem, (beam,), me, member(0, 1))

    def window_copies(beam):
        return [
            remote(
                half.at[beam],
                window_in.at[beam, distance - 1, y_flip],
                window_sem,
                (beam, distance - 1, y_flip),
                behind(-distance if beam == 1 else distance),
                member(y_flip, 0),
            )
            for distance in (2, 3, 1)
            for y_flip in (1, 0)
        ]

    def share_copy(beam):
        rows = pl.ds(pl.multiple_of(core * 64, 64), 64)
        place = spectrum.at[beam, rows]
        return remote(place, place, share_sem, (beam,), me, member(0, 1))

    def leave_copies(beam):
        return [
            remote(
                leavers.at[way, beam],
                arrived.at[beam, :, pl.ds(way * BLOCK, BLOCK)],
                leave_sem,
                (way, beam),
                behind(1 if way == 0 else -1),
                dom,
            )
            for way in range(2)
        ]

    def kick_copies(beam):
        return [
            remote(
                leaver_kicks.at[beam, :, pl.ds((1 - way) * BLOCK, BLOCK)],
                arrived_kicks.at[beam, :, pl.ds(way * BLOCK, BLOCK)],
                kick_sem,
                (way, beam),
                behind(1 if way == 0 else -1),
                dom,
            )
            for way in range(2)
        ]

    def start(copies):
        for copy in copies:
            copy.start()

    def window_send(beam):
        pair_copy(beam).wait_recv()
        mine = pl.ds(pl.multiple_of(core * 64, 64), 64)
        half[beam] = grid[beam, mine, :] + pair_in[beam]
        start(window_copies(beam))

    def share_send(beam):
        for copy in window_copies(beam):
            copy.wait_recv()
        total = window_in[beam, 0, 0]
        for distance in range(SECTIONS):
            for y_flip in (0, 1):
                if distance or y_flip:
                    total = total + window_in[beam, distance, y_flip]
        rows = pl.ds(pl.multiple_of(core * 64, 64), 64)
        spectrum[beam, rows, :] = times_const(total, rights[:, :GRID])
        share_copy(beam).start()

    def solve(beam):
        share_copy(beam).wait_recv()
        scaled = const_times(lefts[:GRID, :], spectrum[beam]) * const[4]
        both = const_times(lefts[GRID:, :], scaled)
        field_x = times_const(both[:GRID], rights[:, :GRID])
        field_y = times_const(both[GRID:], rights[:, GRID:])
        half_grid = GRID // 2
        fields = jnp.concatenate(
            [
                jnp.concatenate([value[:half_grid], value[half_grid:]], axis=1)
                for value in (field_x, field_y)
            ],
            axis=0,
        )
        field[beam] = jnp.concatenate(parts(fields), axis=0)

    row_place = lax.broadcasted_iota(jnp.int32, (BLOCK, 128), 0) * 128 + lax.broadcasted_iota(
        jnp.int32, (BLOCK, 128), 1
    )
    def leave_pack(beam):
        loads["coords", beam].wait()
        for way in range(2):
            rows = slice(ROWS - BLOCK, ROWS) if way == 0 else slice(0, BLOCK)
            limit = (up_count if way == 0 else down_count)[beam]
            base = turn([state[beam, comp, rows, :] for comp in range(4)])
            for comp, value in enumerate((*base, state[beam, 4, rows, :])):
                if way == 0:
                    value = reversed_block(value)
                leavers[way, beam, comp] = jnp.where(row_place < limit, value, 0.0)

    def look_up(beam, first, count):
        rows = pl.ds(pl.multiple_of(first, 8), count)
        kick_x, kick_y = lookup(cell[beam, rows, :], field[1 - beam], pair_levels, row_levels)
        kicks[beam, 0, rows, :] = kick_x
        kicks[beam, 1, rows, :] = kick_y
        shape = (count, 128)
        place = (first + lax.broadcasted_iota(jnp.int32, shape, 0)) * 128
        place = place + lax.broadcasted_iota(jnp.int32, shape, 1)
        stays = (place < ROWS * 128 - counts[beam, 0, 0, 0]) & (place >= counts[beam, 0, 0, 1])
        base = turn([state[beam, comp, rows, :] for comp in range(4)])
        for comp, value in enumerate((*kicked(base, kick_x, kick_y), state[beam, 4, rows, :])):
            kept[beam, comp, rows, :] = jnp.where(stays, value, 0.0)

    def kick_send(beam):
        for comp in range(2):
            down = jnp.where(row_place < down_count[beam], kicks[beam, comp, :BLOCK, :], 0.0)
            up = reversed_block(kicks[beam, comp, ROWS - BLOCK :, :])
            leaver_kicks[beam, comp, :BLOCK, :] = down
            leaver_kicks[beam, comp, BLOCK:, :] = jnp.where(row_place < up_count[beam], up, 0.0)
        start(kick_copies(beam))

    loads["cells", 0].wait()
    loads["weights", 0].wait()
    per_beam = ROWS // DEPOSIT_ROWS

    def deposit_step(i, _):
        beam = i // per_beam
        inner = lax.rem(i, per_beam)

        @pl.when(i == per_beam)
        def _():
            pl.semaphore_wait(barrier, len(partners))
            pair_copy(0).start()
            loads["cells", 1].wait()
            loads["weights", 1].wait()

        @pl.when(i == per_beam + per_beam // 2)
        def _():
            window_send(0)

        rows = pl.ds(pl.multiple_of(inner * DEPOSIT_ROWS, DEPOSIT_ROWS), DEPOSIT_ROWS)
        added = deposit(cell[beam, rows, :], state[beam, 4, rows, :], levels)

        @pl.when(inner == 0)
        def _():
            grid[beam] = added

        @pl.when(inner > 0)
        def _():
            grid[beam] = grid[beam] + added

        return 0

    lax.fori_loop(0, 2 * per_beam, deposit_step, 0)
    pair_copy(1).start()
    loads["counts"].wait()
    up_count = [jnp.where(me == slices - 1, 0, counts[beam, 0, 0, 0]) for beam in range(2)]
    down_count = [jnp.where(me == 0, 0, counts[beam, 0, 0, 1]) for beam in range(2)]
    for beam in range(2):
        leave_pack(beam)
    loads["table"].wait()
    for i in range(3):
        lefts[pl.ds(i * GRID, GRID), :] = left_factor(const[i])
    rights[:, :GRID] = right_factor(const[0])
    rights[:, GRID:] = right_factor(const[3])
    window_send(1)
    share_send(0)
    for beam in range(2):
        start(leave_copies(beam))
    steps = ROWS // 2 // LOOK_ROWS

    def look_step(i, _):
        part = i // steps
        inner = lax.rem(i, steps)
        beam = 1 - lax.rem(part, 2)

        @pl.when((inner == 0) & (part < 2))
        def _():
            solve(1 - beam)

        @pl.when(i == steps // 2)
        def _():
            share_send(1)

        @pl.when(i == steps)
        def _():
            kick_send(1)

        @pl.when(i == 2 * steps)
        def _():
            kick_send(0)

        ends = inner * LOOK_ROWS + jnp.where(inner * LOOK_ROWS >= BLOCK, ROWS - 2 * BLOCK, 0)
        middle = BLOCK + inner * LOOK_ROWS
        look_up(beam, jnp.where(part < 2, ends, middle), LOOK_ROWS)
        return 0

    lax.fori_loop(0, 4 * steps, look_step, 0)
    for beam in range(2):
        for copy in (*leave_copies(beam), *kick_copies(beam)):
            copy.wait()
        for copy in (pair_copy(beam), *window_copies(beam), share_copy(beam)):
            copy.wait_send()


def finish(kept_in, arrived, arrived_kicks, kept, arrivals):
    for beam in range(2):
        kept[beam] = kept_in[beam]
        base = [arrived[beam, comp] for comp in range(4)]
        done = kicked(base, arrived_kicks[beam, 0], arrived_kicks[beam, 1])
        for comp, value in enumerate((*done, arrived[beam, 4])):
            arrivals[beam, comp] = value


def local(slices, particles, cells, counts):
    in_hbm = pl.BlockSpec(memory_space=pltpu.HBM)
    dma = pltpu.SemaphoreType.DMA
    in_vmem = pl.BlockSpec(memory_space=pltpu.VMEM)
    shapes = (
        jax.ShapeDtypeStruct((2, 5, ROWS, 128), F32),
        jax.ShapeDtypeStruct((2, 5, 2 * BLOCK, 128), F32),
    )
    results = pl.pallas_call(
        functools.partial(kernel, slices),
        out_shape=(*shapes, jax.ShapeDtypeStruct((2, 2, 2 * BLOCK, 128), F32)),
        in_specs=[
            in_hbm,
            in_hbm,
            in_hbm,
            in_hbm,
        ],
        out_specs=(in_vmem, in_vmem, in_vmem),
        scratch_shapes=[
            pltpu.VMEM((2, 5, ROWS, 128), F32),
            pltpu.VMEM((2, ROWS, 128), jnp.int32),
            pltpu.VMEM((5, GRID, GRID), F32),
            pltpu.VMEM((3 * GRID, 3 * GRID), BF16),
            pltpu.VMEM((3 * GRID, 2 * GRID), BF16),
            pltpu.SMEM((2, 1, 1, 2), jnp.int32),
            pltpu.VMEM((2, GRID, GRID), F32),
            pltpu.VMEM((2, GRID // 2, GRID), F32),
            pltpu.VMEM((2, GRID // 2, GRID), F32),
            pltpu.VMEM((2, SECTIONS, 2, GRID // 2, GRID), F32),
            pltpu.VMEM((2, GRID, GRID), F32),
            pltpu.VMEM((2, 2 * GRID, 2 * GRID), BF16),
            pltpu.VMEM((2, 2, 5, BLOCK, 128), F32),
            pltpu.VMEM((2, 2, ROWS, 128), F32),
            pltpu.VMEM((2, 2, 2 * BLOCK, 128), F32),
            dma((8,)),
            dma((2, 2)),
            dma((2, 2, SECTIONS, 2)),
            dma((2, 2)),
            dma((2, 2, 2)),
            dma((2, 2, 2)),
        ],
        compiler_params=pltpu.CompilerParams(
            collective_id=0, has_side_effects=True, vmem_limit_bytes=40 * 2**20
        ),
        cost_estimate=pl.CostEstimate(
            flops=7 * 10**9, bytes_accessed=2 * 10**6, transcendentals=0
        ),
        name="crossing",
    )(
        pltpu.with_memory_space_constraint(particles.reshape(2, 5, ROWS, 128), pltpu.HBM),
        pltpu.with_memory_space_constraint(cells.reshape(2, ROWS, 128), pltpu.HBM),
        pltpu.with_memory_space_constraint(counts.transpose(0, 2, 3, 1), pltpu.HBM),
        pltpu.with_memory_space_constraint(jnp.asarray(constants()), pltpu.HBM),
    )
    kept, arrivals = pl.pallas_call(
        finish,
        out_shape=shapes,
        in_specs=[in_vmem, in_vmem, in_vmem],
        out_specs=(in_vmem, in_vmem),
        name="finish",
    )(*(pltpu.with_memory_space_constraint(result, pltpu.VMEM) for result in results))
    return kept.reshape(2, 5, 1, ROWS * 128), arrivals.reshape(2, 5, 1, 2 * BLOCK * 128)


def solution(mesh):
    return jax.shard_map(
        functools.partial(local, mesh.shape["cuts"]),
        mesh=mesh,
        in_specs=(
            P(None, None, "cuts", "dom"),
            P(None, "cuts", "dom"),
            P(None, None, "cuts", "dom"),
        ),
        out_specs=(P(None, None, "cuts", "dom"), P(None, None, "cuts", "dom")),
        check_vma=False,
    )
```

time: 40.1 us -> 34.4 us (0.86)
  Pallas kernels: 37.8 us -> 33.6 us
  local copies, waits for them, and re-layouts: 1.57 us -> 0 us
    pallas_call x2, Pallas kernels: 37.8 us -> 33.6 us  [the longest x1 32.6 us: local(): pl.pallas_call(functools.partial(kernel, slices), out_shape=(*shapes, jax...]
    unnamed x4 -> x0, local copies, waits for them, and re-layouts: 1.57 us -> none
where the time goes in v3:
time: 34.4 us; the launch traced here: 34.3 us
  Pallas kernels  33.6 us (98%)
  between operations  0.64 us (2%)
    pallas_call x1, Pallas kernels, local(): pl.pallas_call(functools.partial(kernel, slices), out_shape=(*shapes, jax...  32.6 us
    pallas_call x1, Pallas kernels, local(): pl.pallas_call(finish, out_shape=shapes, in_specs=[in_vmem, in_vmem, in_v...  1.02 us

profile of v3, /device:TPU:1, one launch (start us, length us, event | category | flops | bytes accessed | tf_op | source)
XLA Modules:
  0.0 34.3 jit_solution(6345943160454518391)
XLA Ops:
  0.6 32.6 %crossing.1 = (f32[2,5,128,128]{3,2,1,0:T(8,128)S(1)}, f32[2,5,64,128]{3,2,1,0:T(8,128)S(1)}, f32[2,2,64,128]{3,2,1,0:T(8,128)S(1)}) custom-call(f32[2,5,128,128]{3,2,1,0:T(8,128)} %bitcast.7, s32[2,128,128]{2,1,0:T(8,128)} %bitcast.10, s32[2,1,1,2]{3,2,1,0:T(1,128)} %bitcast.11, f32[5,128,128]{2,1,0:T(8,128)} %constant.2.clone.table), custom_call_target="tpu_custom_call" | custom-call | flops 7000000000 | bytes 2000000 | tf_op jit(solution)/shard_map/crossing/pallas_call | solution.py:440
  33.2 1.0 %finish.1 = (f32[2,5,128,128]{3,2,1,0:T(8,128)}, f32[2,5,64,128]{3,2,1,0:T(8,128)}) custom-call(f32[2,5,128,128]{3,2,1,0:T(8,128)S(1)} %get-tuple-element.7.kept_in, f32[2,5,64,128]{3,2,1,0:T(8,128)S(1)} %get-tuple-element.8.arrived, f32[2,2,64,128]{3,2,1,0:T(8,128)S(1)} %get-tuple-element.9.arrived_kicks), custom_call_target="tpu_custom_call" | custom-call | tf_op jit(solution)/shard_map/finish/pallas_call | solution.py:486

commit v4 on v3

--- a/solution.py
+++ b/solution.py
@@ -185,13 +185,18 @@
         )
         return copy
 
+    ring = slices // 2
+    place_in_ring = lax.rem(me, ring)
+    lead = jnp.where(place_in_ring < ring // 2, 1, 0)
+    use_first = lead
     loads = {}
-    for beam in (0, 1):
-        loads["cells", beam] = pltpu.make_async_copy(
-            cells.at[beam], cell.at[beam], in_sem.at[beam]
+    for turn_no in range(2):
+        beam = lead if turn_no == 0 else 1 - lead
+        loads["cells", turn_no] = pltpu.make_async_copy(
+            cells.at[beam], cell.at[beam], in_sem.at[turn_no]
         )
-        loads["weights", beam] = pltpu.make_async_copy(
-            particles.at[beam, 4], state.at[beam, 4], in_sem.at[2 + beam]
+        loads["weights", turn_no] = pltpu.make_async_copy(
+            particles.at[beam, 4], state.at[beam, 4], in_sem.at[2 + turn_no]
         )
     for beam in (0, 1):
         loads["coords", beam] = pltpu.make_async_copy(
@@ -225,7 +230,7 @@
                 window_in.at[beam, distance - 1, y_flip],
                 window_sem,
                 (beam, distance - 1, y_flip),
-                behind(-distance if beam == 1 else distance),
+                behind(distance * (1 - 2 * beam)),
                 member(y_flip, 0),
             )
             for distance in (2, 3, 1)
@@ -304,11 +309,15 @@
     row_place = lax.broadcasted_iota(jnp.int32, (BLOCK, 128), 0) * 128 + lax.broadcasted_iota(
         jnp.int32, (BLOCK, 128), 1
     )
+    def leaver_counts(beam):
+        up = jnp.where(me == slices - 1, 0, counts[beam, 0, 0, 0])
+        return up, jnp.where(me == 0, 0, counts[beam, 0, 0, 1])
+
     def leave_pack(beam):
         loads["coords", beam].wait()
         for way in range(2):
             rows = slice(ROWS - BLOCK, ROWS) if way == 0 else slice(0, BLOCK)
-            limit = (up_count if way == 0 else down_count)[beam]
+            limit = leaver_counts(beam)[way]
             base = turn([state[beam, comp, rows, :] for comp in range(4)])
             for comp, value in enumerate((*base, state[beam, 4, rows, :])):
                 if way == 0:
@@ -329,11 +338,12 @@
             kept[beam, comp, rows, :] = jnp.where(stays, value, 0.0)
 
     def kick_send(beam):
+        up_count, down_count = leaver_counts(beam)
         for comp in range(2):
-            down = jnp.where(row_place < down_count[beam], kicks[beam, comp, :BLOCK, :], 0.0)
+            down = jnp.where(row_place < down_count, kicks[beam, comp, :BLOCK, :], 0.0)
             up = reversed_block(kicks[beam, comp, ROWS - BLOCK :, :])
             leaver_kicks[beam, comp, :BLOCK, :] = down
-            leaver_kicks[beam, comp, BLOCK:, :] = jnp.where(row_place < up_count[beam], up, 0.0)
+            leaver_kicks[beam, comp, BLOCK:, :] = jnp.where(row_place < up_count, up, 0.0)
         start(kick_copies(beam))
 
     loads["cells", 0].wait()
@@ -341,19 +351,19 @@
     per_beam = ROWS // DEPOSIT_ROWS
 
     def deposit_step(i, _):
-        beam = i // per_beam
+        beam = jnp.where(i < per_beam, lead, 1 - lead)
         inner = lax.rem(i, per_beam)
 
         @pl.when(i == per_beam)
         def _():
             pl.semaphore_wait(barrier, len(partners))
-            pair_copy(0).start()
+            pair_copy(lead).start()
             loads["cells", 1].wait()
             loads["weights", 1].wait()
 
         @pl.when(i == per_beam + per_beam // 2)
         def _():
-            window_send(0)
+            window_send(lead)
 
         rows = pl.ds(pl.multiple_of(inner * DEPOSIT_ROWS, DEPOSIT_ROWS), DEPOSIT_ROWS)
         added = deposit(cell[beam, rows, :], state[beam, 4, rows, :], levels)
@@ -369,19 +379,17 @@
         return 0
 
     lax.fori_loop(0, 2 * per_beam, deposit_step, 0)
-    pair_copy(1).start()
-    loads["counts"].wait()
-    up_count = [jnp.where(me == slices - 1, 0, counts[beam, 0, 0, 0]) for beam in range(2)]
-    down_count = [jnp.where(me == 0, 0, counts[beam, 0, 0, 1]) for beam in range(2)]
-    for beam in range(2):
-        leave_pack(beam)
+    pair_copy(1 - lead).start()
     loads["table"].wait()
     for i in range(3):
         lefts[pl.ds(i * GRID, GRID), :] = left_factor(const[i])
     rights[:, :GRID] = right_factor(const[0])
     rights[:, GRID:] = right_factor(const[3])
-    window_send(1)
-    share_send(0)
+    window_send(1 - lead)
+    loads["counts"].wait()
+    for beam in range(2):
+        leave_pack(beam)
+    share_send(use_first)
     for beam in range(2):
         start(leave_copies(beam))
     steps = ROWS // 2 // LOOK_ROWS
@@ -389,7 +397,7 @@
     def look_step(i, _):
         part = i // steps
         inner = lax.rem(i, steps)
-        beam = 1 - lax.rem(part, 2)
+        beam = jnp.where(lax.rem(part, 2) == 0, 1 - use_first, use_first)
 
         @pl.when((inner == 0) & (part < 2))
         def _():
@@ -397,15 +405,15 @@
 
         @pl.when(i == steps // 2)
         def _():
-            share_send(1)
+            share_send(1 - use_first)
 
         @pl.when(i == steps)
         def _():
-            kick_send(1)
+            kick_send(1 - use_first)
 
         @pl.when(i == 2 * steps)
         def _():
-            kick_send(0)
+            kick_send(use_first)
 
         ends = inner * LOOK_ROWS + jnp.where(inner * LOOK_ROWS >= BLOCK, ROWS - 2 * BLOCK, 0)
         middle = BLOCK + inner * LOOK_ROWS

time: 34.4 us -> 32.4 us (0.942)
  Pallas kernels: 33.6 us -> 31.7 us
    pallas_call x1, Pallas kernels: 32.6 us -> 30.7 us  [local(): pl.pallas_call(functools.partial(kernel, slices), out_shape=(*shapes, jax...]
where the time goes in v4:
time: 32.4 us; the launch traced here: 32.3 us
  Pallas kernels  31.7 us (98%)
  between operations  0.64 us (2%)
    pallas_call x1, Pallas kernels, local(): pl.pallas_call(functools.partial(kernel, slices), out_shape=(*shapes, jax...  30.7 us
    pallas_call x1, Pallas kernels, local(): pl.pallas_call(finish, out_shape=shapes, in_specs=[in_vmem, in_vmem, in_v...  1.02 us

profile of v4, /device:TPU:1, one launch (start us, length us, event | category | flops | bytes accessed | tf_op | source)
XLA Modules:
  0.0 32.3 jit_solution(9731899234267146673)
XLA Ops:
  0.6 30.7 %crossing.1 = (f32[2,5,128,128]{3,2,1,0:T(8,128)S(1)}, f32[2,5,64,128]{3,2,1,0:T(8,128)S(1)}, f32[2,2,64,128]{3,2,1,0:T(8,128)S(1)}) custom-call(f32[2,5,128,128]{3,2,1,0:T(8,128)} %bitcast.7, s32[2,128,128]{2,1,0:T(8,128)} %bitcast.10, s32[2,1,1,2]{3,2,1,0:T(1,128)} %bitcast.11, f32[5,128,128]{2,1,0:T(8,128)} %constant.2.clone.table), custom_call_target="tpu_custom_call" | custom-call | flops 7000000000 | bytes 2000000 | tf_op jit(solution)/shard_map/crossing/pallas_call | solution.py:448
  31.3 1.0 %finish.1 = (f32[2,5,128,128]{3,2,1,0:T(8,128)}, f32[2,5,64,128]{3,2,1,0:T(8,128)}) custom-call(f32[2,5,128,128]{3,2,1,0:T(8,128)S(1)} %get-tuple-element.7.kept_in, f32[2,5,64,128]{3,2,1,0:T(8,128)S(1)} %get-tuple-element.8.arrived, f32[2,2,64,128]{3,2,1,0:T(8,128)S(1)} %get-tuple-element.9.arrived_kicks), custom_call_target="tpu_custom_call" | custom-call | tf_op jit(solution)/shard_map/finish/pallas_call | solution.py:494

commit v5 on v4

--- a/solution.py
+++ b/solution.py
@@ -15,7 +15,6 @@
 ROWS = 128
 BLOCK = 32
 DEPOSIT_ROWS = 64
-LOOK_ROWS = 32
 KICK_SCALE = 0.01
 COS_X, SIN_X = (math.cos(2 * math.pi * 0.31), math.sin(2 * math.pi * 0.31))
 COS_Y, SIN_Y = (math.cos(2 * math.pi * 0.32), math.sin(2 * math.pi * 0.32))
@@ -189,6 +188,7 @@
     place_in_ring = lax.rem(me, ring)
     lead = jnp.where(place_in_ring < ring // 2, 1, 0)
     use_first = lead
+    second = jnp.where(place_in_ring >= ring // 2, 2, 3)
     loads = {}
     for turn_no in range(2):
         beam = lead if turn_no == 0 else 1 - lead
@@ -255,18 +255,15 @@
             for way in range(2)
         ]
 
-    def kick_copies(beam):
-        return [
-            remote(
-                leaver_kicks.at[beam, :, pl.ds((1 - way) * BLOCK, BLOCK)],
-                arrived_kicks.at[beam, :, pl.ds(way * BLOCK, BLOCK)],
-                kick_sem,
-                (way, beam),
-                behind(1 if way == 0 else -1),
-                dom,
-            )
-            for way in range(2)
-        ]
+    def kick_copy(beam, way):
+        return remote(
+            leaver_kicks.at[beam, :, pl.ds((1 - way) * BLOCK, BLOCK)],
+            arrived_kicks.at[beam, :, pl.ds(way * BLOCK, BLOCK)],
+            kick_sem,
+            (way, beam),
+            behind(1 if way == 0 else -1),
+            dom,
+        )
 
     def start(copies):
         for copy in copies:
@@ -337,14 +334,16 @@
         for comp, value in enumerate((*kicked(base, kick_x, kick_y), state[beam, 4, rows, :])):
             kept[beam, comp, rows, :] = jnp.where(stays, value, 0.0)
 
-    def kick_send(beam):
-        up_count, down_count = leaver_counts(beam)
+    def kick_send(beam, way):
+        limit = leaver_counts(beam)[way]
+        rows = slice(ROWS - BLOCK, ROWS) if way == 0 else slice(0, BLOCK)
+        place = slice((1 - way) * BLOCK, (2 - way) * BLOCK)
         for comp in range(2):
-            down = jnp.where(row_place < down_count, kicks[beam, comp, :BLOCK, :], 0.0)
-            up = reversed_block(kicks[beam, comp, ROWS - BLOCK :, :])
-            leaver_kicks[beam, comp, :BLOCK, :] = down
-            leaver_kicks[beam, comp, BLOCK:, :] = jnp.where(row_place < up_count, up, 0.0)
-        start(kick_copies(beam))
+            kick = kicks[beam, comp, rows, :]
+            if way == 0:
+                kick = reversed_block(kick)
+            leaver_kicks[beam, comp, place, :] = jnp.where(row_place < limit, kick, 0.0)
+        kick_copy(beam, way).start()
 
     loads["cells", 0].wait()
     loads["weights", 0].wait()
@@ -392,37 +391,36 @@
     share_send(use_first)
     for beam in range(2):
         start(leave_copies(beam))
-    steps = ROWS // 2 // LOOK_ROWS
 
     def look_step(i, _):
-        part = i // steps
-        inner = lax.rem(i, steps)
-        beam = jnp.where(lax.rem(part, 2) == 0, 1 - use_first, use_first)
-
-        @pl.when((inner == 0) & (part < 2))
-        def _():
-            solve(1 - beam)
-
-        @pl.when(i == steps // 2)
+        now = jnp.where((i == second) | (i == second + 1) | (i > 5), use_first, 1 - use_first)
+        block = jnp.where((i == 5) | (i == 7), 2, 1)
+        block = jnp.where((i == 1) | (i == second + 1), 0, block)
+        block = jnp.where((i == 0) | (i == second), 3, block)
+        before = jnp.where(i > second, use_first, 1 - use_first)
+
+        @pl.when((i == 0) | (i == second))
+        def _():
+            solve(1 - now)
+
+        @pl.when(i == second - 1)
         def _():
             share_send(1 - use_first)
 
-        @pl.when(i == steps)
-        def _():
-            kick_send(1 - use_first)
-
-        @pl.when(i == 2 * steps)
-        def _():
-            kick_send(use_first)
-
-        ends = inner * LOOK_ROWS + jnp.where(inner * LOOK_ROWS >= BLOCK, ROWS - 2 * BLOCK, 0)
-        middle = BLOCK + inner * LOOK_ROWS
-        look_up(beam, jnp.where(part < 2, ends, middle), LOOK_ROWS)
+        @pl.when((i == 1) | (i == second + 1))
+        def _():
+            kick_send(before, 0)
+
+        @pl.when((i == 2) | (i == second + 2))
+        def _():
+            kick_send(before, 1)
+
+        look_up(now, block * BLOCK, BLOCK)
         return 0
 
-    lax.fori_loop(0, 4 * steps, look_step, 0)
+    lax.fori_loop(0, 8, look_step, 0)
     for beam in range(2):
-        for copy in (*leave_copies(beam), *kick_copies(beam)):
+        for copy in (*leave_copies(beam), kick_copy(beam, 0), kick_copy(beam, 1)):
             copy.wait()
         for copy in (pair_copy(beam), *window_copies(beam), share_copy(beam)):
             copy.wait_send()

time: 32.4 us -> 31.6 us (0.975)
  Pallas kernels: 31.7 us -> 30.9 us
    pallas_call x1, Pallas kernels: 30.7 us -> 29.9 us  [local(): pl.pallas_call(functools.partial(kernel, slices), out_shape=(*shapes, jax...]
where the time goes in v5:
time: 31.6 us; the launch traced here: 31.5 us
  Pallas kernels  30.9 us (98%)
  between operations  0.64 us (2%)
    pallas_call x1, Pallas kernels, local(): pl.pallas_call(functools.partial(kernel, slices), out_shape=(*shapes, jax...  29.9 us
    pallas_call x1, Pallas kernels, local(): pl.pallas_call(finish, out_shape=shapes, in_specs=[in_vmem, in_vmem, in_v...  1.02 us

profile of v5, /device:TPU:1, one launch (start us, length us, event | category | flops | bytes accessed | tf_op | source)
XLA Modules:
  0.0 31.5 jit_solution(14790753397940525634)
XLA Ops:
  0.6 29.9 %crossing.1 = (f32[2,5,128,128]{3,2,1,0:T(8,128)S(1)}, f32[2,5,64,128]{3,2,1,0:T(8,128)S(1)}, f32[2,2,64,128]{3,2,1,0:T(8,128)S(1)}) custom-call(f32[2,5,128,128]{3,2,1,0:T(8,128)} %bitcast.7, s32[2,128,128]{2,1,0:T(8,128)} %bitcast.10, s32[2,1,1,2]{3,2,1,0:T(1,128)} %bitcast.11, f32[5,128,128]{2,1,0:T(8,128)} %constant.2.clone.table), custom_call_target="tpu_custom_call" | custom-call | flops 7000000000 | bytes 2000000 | tf_op jit(solution)/shard_map/crossing/pallas_call | solution.py:446
  30.5 1.0 %finish.1 = (f32[2,5,128,128]{3,2,1,0:T(8,128)}, f32[2,5,64,128]{3,2,1,0:T(8,128)}) custom-call(f32[2,5,128,128]{3,2,1,0:T(8,128)S(1)} %get-tuple-element.7.kept_in, f32[2,5,64,128]{3,2,1,0:T(8,128)S(1)} %get-tuple-element.8.arrived, f32[2,2,64,128]{3,2,1,0:T(8,128)S(1)} %get-tuple-element.9.arrived_kicks), custom_call_target="tpu_custom_call" | custom-call | tf_op jit(solution)/shard_map/finish/pallas_call | solution.py:492

commit v6 on v5

--- a/solution.py
+++ b/solution.py
@@ -60,23 +60,28 @@
     return jnp.broadcast_to(row, (GRID, 128))
 
 
-def deposit(cells, weights, levels):
-    row = (cells >> 7).astype(F32).astype(BF16)
+def deposit(cells, weights, first_row, levels):
+    half_grid = GRID // 2
+    row = ((cells >> 7) - first_row).astype(F32).astype(BF16)
     column = (cells & 127).astype(F32).astype(BF16)
     high, low = parts(weights)
     zero, one = jnp.zeros((GRID, 128), BF16), jnp.ones((GRID, 128), BF16)
     hit_column, part_high, part_low = [], [], []
+
+    def half_rows(value):
+        return jnp.broadcast_to(value, (half_grid, 128))
+
     for i in range(cells.shape[0]):
-        here = levels == across(row[i : i + 1])
-        part_high.append(jnp.where(here, across(high[i : i + 1]), zero))
-        part_low.append(jnp.where(here, across(low[i : i + 1]), zero))
+        here = levels[:half_grid] == half_rows(row[i : i + 1])
+        part_high.append(jnp.where(here, half_rows(high[i : i + 1]), zero[:half_grid]))
+        part_low.append(jnp.where(here, half_rows(low[i : i + 1]), zero[:half_grid]))
         hit_column.append(jnp.where(levels == across(column[i : i + 1]), one, zero))
     left = jnp.concatenate(
         [jnp.concatenate(part_high, axis=1), jnp.concatenate(part_low, axis=1)], axis=0
     )
     right = jnp.concatenate(hit_column, axis=1)
     both = lax.dot_general(left, right, (((1,), (1,)), ((), ())), preferred_element_type=F32)
-    return both[:GRID] + both[GRID:]
+    return both[:half_grid] + both[half_grid:]
 
 
 def lookup(cells, field, levels, row_levels):
@@ -146,7 +151,7 @@
     rights,
     counts,
     grid,
-    pair_in,
+    scatter_in,
     half,
     window_in,
     spectrum,
@@ -155,7 +160,7 @@
     kicks,
     leaver_kicks,
     in_sem,
-    pair_sem,
+    scatter_sem,
     window_sem,
     share_sem,
     leave_sem,
@@ -208,33 +213,47 @@
         load.start()
 
     barrier = pltpu.get_barrier_semaphore()
-    partners = [(me, member(0, 1))]
+    partners = [(me, member(0, 1)), (me, member(1, 0)), (me, member(1, 1))]
     for distance in range(1, SECTIONS + 1):
         for sign in (1, -1):
-            for y_flip in (0, 1):
-                partners.append((behind(sign * distance), member(y_flip, 0)))
+            partners.append((behind(sign * distance), dom))
     for partner in partners:
         pl.semaphore_signal(barrier, inc=1, device_id=partner, device_id_type=MESH)
 
     pair_levels = lax.broadcasted_iota(jnp.int32, (2 * GRID, 128), 0).astype(F32).astype(BF16)
     levels = pair_levels[:GRID]
     row_levels = lax.broadcasted_iota(jnp.int32, (GRID // 2, 128), 0)
-    def pair_copy(beam):
+    def other_half_copies(beam):
         other = pl.ds(pl.multiple_of((1 - core) * 64, 64), 64)
-        return remote(grid.at[beam, other], pair_in.at[beam], pair_sem, (beam,), me, member(0, 1))
+        return [
+            remote(
+                grid.at[beam, other],
+                scatter_in.at[beam, 2 * y_flip],
+                scatter_sem,
+                (beam, 2 * y_flip),
+                me,
+                member(y_flip, 1),
+            )
+            for y_flip in (1, 0)
+        ]
+
+    def own_half_copy(beam):
+        mine = pl.ds(pl.multiple_of(core * 64, 64), 64)
+        return remote(
+            grid.at[beam, mine], scatter_in.at[beam, 1], scatter_sem, (beam, 1), me, member(1, 0)
+        )
 
     def window_copies(beam):
         return [
             remote(
                 half.at[beam],
-                window_in.at[beam, distance - 1, y_flip],
+                window_in.at[beam, distance - 1],
                 window_sem,
-                (beam, distance - 1, y_flip),
+                (beam, distance - 1),
                 behind(distance * (1 - 2 * beam)),
-                member(y_flip, 0),
+                dom,
             )
             for distance in (2, 3, 1)
-            for y_flip in (1, 0)
         ]
 
     def share_copy(beam):
@@ -270,19 +289,20 @@
             copy.start()
 
     def window_send(beam):
-        pair_copy(beam).wait_recv()
+        for copy in (*other_half_copies(beam), own_half_copy(beam)):
+            copy.wait_recv()
         mine = pl.ds(pl.multiple_of(core * 64, 64), 64)
-        half[beam] = grid[beam, mine, :] + pair_in[beam]
+        half[beam] = (grid[beam, mine, :] + scatter_in[beam, 0]) + (
+            scatter_in[beam, 1] + scatter_in[beam, 2]
+        )
         start(window_copies(beam))
 
     def share_send(beam):
         for copy in window_copies(beam):
             copy.wait_recv()
-        total = window_in[beam, 0, 0]
-        for distance in range(SECTIONS):
-            for y_flip in (0, 1):
-                if distance or y_flip:
-                    total = total + window_in[beam, distance, y_flip]
+        total = window_in[beam, 0]
+        for distance in range(1, SECTIONS):
+            total = total + window_in[beam, distance]
         rows = pl.ds(pl.multiple_of(core * 64, 64), 64)
         spectrum[beam, rows, :] = times_const(total, rights[:, :GRID])
         share_copy(beam).start()
@@ -347,47 +367,56 @@
 
     loads["cells", 0].wait()
     loads["weights", 0].wait()
-    per_beam = ROWS // DEPOSIT_ROWS
+    per_half = ROWS // DEPOSIT_ROWS
+    per_beam = 2 * per_half
 
     def deposit_step(i, _):
         beam = jnp.where(i < per_beam, lead, 1 - lead)
-        inner = lax.rem(i, per_beam)
+        own = lax.rem(i // per_half, 2)
+        inner = lax.rem(i, per_half)
+
+        @pl.when(i == per_half + 1)
+        def _():
+            pl.semaphore_wait(barrier, len(partners))
+            start(other_half_copies(lead))
 
         @pl.when(i == per_beam)
         def _():
-            pl.semaphore_wait(barrier, len(partners))
-            pair_copy(lead).start()
+            own_half_copy(lead).start()
             loads["cells", 1].wait()
             loads["weights", 1].wait()
 
-        @pl.when(i == per_beam + per_beam // 2)
-        def _():
-            window_send(lead)
+        @pl.when(i == per_beam + per_half)
+        def _():
+            start(other_half_copies(1 - lead))
 
         rows = pl.ds(pl.multiple_of(inner * DEPOSIT_ROWS, DEPOSIT_ROWS), DEPOSIT_ROWS)
-        added = deposit(cell[beam, rows, :], state[beam, 4, rows, :], levels)
+        first_row = jnp.where(own == 1, core, 1 - core) * 64
+        place = pl.ds(pl.multiple_of(first_row, 64), 64)
+        added = deposit(cell[beam, rows, :], state[beam, 4, rows, :], first_row, levels)
 
         @pl.when(inner == 0)
         def _():
-            grid[beam] = added
+            grid[beam, place, :] = added
 
         @pl.when(inner > 0)
         def _():
-            grid[beam] = grid[beam] + added
+            grid[beam, place, :] = grid[beam, place, :] + added
 
         return 0
 
     lax.fori_loop(0, 2 * per_beam, deposit_step, 0)
-    pair_copy(1 - lead).start()
+    own_half_copy(1 - lead).start()
     loads["table"].wait()
     for i in range(3):
         lefts[pl.ds(i * GRID, GRID), :] = left_factor(const[i])
     rights[:, :GRID] = right_factor(const[0])
     rights[:, GRID:] = right_factor(const[3])
-    window_send(1 - lead)
+    window_send(lead)
     loads["counts"].wait()
     for beam in range(2):
         leave_pack(beam)
+    window_send(1 - lead)
     share_send(use_first)
     for beam in range(2):
         start(leave_copies(beam))
@@ -422,7 +451,8 @@
     for beam in range(2):
         for copy in (*leave_copies(beam), kick_copy(beam, 0), kick_copy(beam, 1)):
             copy.wait()
-        for copy in (pair_copy(beam), *window_copies(beam), share_copy(beam)):
+        scatter = (*other_half_copies(beam), own_half_copy(beam))
+        for copy in (*scatter, *window_copies(beam), share_copy(beam)):
             copy.wait_send()
 
 
@@ -461,17 +491,17 @@
             pltpu.VMEM((3 * GRID, 2 * GRID), BF16),
             pltpu.SMEM((2, 1, 1, 2), jnp.int32),
             pltpu.VMEM((2, GRID, GRID), F32),
+            pltpu.VMEM((2, 3, GRID // 2, GRID), F32),
             pltpu.VMEM((2, GRID // 2, GRID), F32),
-            pltpu.VMEM((2, GRID // 2, GRID), F32),
-            pltpu.VMEM((2, SECTIONS, 2, GRID // 2, GRID), F32),
+            pltpu.VMEM((2, SECTIONS, GRID // 2, GRID), F32),
             pltpu.VMEM((2, GRID, GRID), F32),
             pltpu.VMEM((2, 2 * GRID, 2 * GRID), BF16),
             pltpu.VMEM((2, 2, 5, BLOCK, 128), F32),
             pltpu.VMEM((2, 2, ROWS, 128), F32),
             pltpu.VMEM((2, 2, 2 * BLOCK, 128), F32),
             dma((8,)),
-            dma((2, 2)),
-            dma((2, 2, SECTIONS, 2)),
+            dma((2, 2, 3)),
+            dma((2, 2, SECTIONS)),
             dma((2, 2)),
             dma((2, 2, 2)),
             dma((2, 2, 2)),

time: 31.6 us -> 31 us (0.981)
  Pallas kernels: 30.9 us -> 30.3 us
    pallas_call x1, Pallas kernels: 29.9 us -> 29.2 us  [local(): pl.pallas_call(functools.partial(kernel, slices), out_shape=(*shapes, jax...]
where the time goes in v6:
time: 31 us; the launch traced here: 30.9 us
  Pallas kernels  30.3 us (98%)
  between operations  0.64 us (2%)
    pallas_call x1, Pallas kernels, local(): pl.pallas_call(functools.partial(kernel, slices), out_shape=(*shapes, jax...  29.2 us
    pallas_call x1, Pallas kernels, local(): pl.pallas_call(finish, out_shape=shapes, in_specs=[in_vmem, in_vmem, in_v...  1.02 us

profile of v6, /device:TPU:1, one launch (start us, length us, event | category | flops | bytes accessed | tf_op | source)
XLA Modules:
  0.0 30.9 jit_solution(3929441701386707074)
XLA Ops:
  0.6 29.2 %crossing.1 = (f32[2,5,128,128]{3,2,1,0:T(8,128)S(1)}, f32[2,5,64,128]{3,2,1,0:T(8,128)S(1)}, f32[2,2,64,128]{3,2,1,0:T(8,128)S(1)}) custom-call(f32[2,5,128,128]{3,2,1,0:T(8,128)} %bitcast.7, s32[2,128,128]{2,1,0:T(8,128)} %bitcast.10, s32[2,1,1,2]{3,2,1,0:T(1,128)} %bitcast.11, f32[5,128,128]{2,1,0:T(8,128)} %constant.2.clone.table), custom_call_target="tpu_custom_call" | custom-call | flops 7000000000 | bytes 2000000 | tf_op jit(solution)/shard_map/crossing/pallas_call | solution.py:476
  29.9 1.0 %finish.1 = (f32[2,5,128,128]{3,2,1,0:T(8,128)}, f32[2,5,64,128]{3,2,1,0:T(8,128)}) custom-call(f32[2,5,128,128]{3,2,1,0:T(8,128)S(1)} %get-tuple-element.7.kept_in, f32[2,5,64,128]{3,2,1,0:T(8,128)S(1)} %get-tuple-element.8.arrived, f32[2,2,64,128]{3,2,1,0:T(8,128)S(1)} %get-tuple-element.9.arrived_kicks), custom_call_target="tpu_custom_call" | custom-call | tf_op jit(solution)/shard_map/finish/pallas_call | solution.py:522

commit v7 on v6

--- a/solution.py
+++ b/solution.py
@@ -193,7 +193,7 @@
     place_in_ring = lax.rem(me, ring)
     lead = jnp.where(place_in_ring < ring // 2, 1, 0)
     use_first = lead
-    second = jnp.where(place_in_ring >= ring // 2, 2, 3)
+    second = jnp.where(place_in_ring >= 0, 2, 3)
     loads = {}
     for turn_no in range(2):
         beam = lead if turn_no == 0 else 1 - lead
@@ -447,7 +447,14 @@
         look_up(now, block * BLOCK, BLOCK)
         return 0
 
-    lax.fori_loop(0, 8, look_step, 0)
+    lax.fori_loop(0, 5, look_step, 0)
+
+    @pl.when(second == 3)
+    def _():
+        kick_send(use_first, 1)
+
+    look_up(1 - use_first, 2 * BLOCK, BLOCK)
+    look_up(use_first, BLOCK, 2 * BLOCK)
     for beam in range(2):
         for copy in (*leave_copies(beam), kick_copy(beam, 0), kick_copy(beam, 1)):
             copy.wait()

time: 31 us -> 31 us (level)
  no operation moved by 1% of the time
where the time goes in v7:
time: 31 us; the launch traced here: 30.9 us
  Pallas kernels  30.2 us (97%)
  between operations  0.64 us (2%)
    pallas_call x1, Pallas kernels, local(): pl.pallas_call(functools.partial(kernel, slices), out_shape=(*shapes, jax...  29.2 us
    pallas_call x1, Pallas kernels, local(): pl.pallas_call(finish, out_shape=shapes, in_specs=[in_vmem, in_vmem, in_v...  1.02 us

profile of v7, /device:TPU:1, one launch (start us, length us, event | category | flops | bytes accessed | tf_op | source)
XLA Modules:
  0.0 30.9 jit_solution(221238505777004842)
XLA Ops:
  0.6 29.2 %crossing.1 = (f32[2,5,128,128]{3,2,1,0:T(8,128)S(1)}, f32[2,5,64,128]{3,2,1,0:T(8,128)S(1)}, f32[2,2,64,128]{3,2,1,0:T(8,128)S(1)}) custom-call(f32[2,5,128,128]{3,2,1,0:T(8,128)} %bitcast.7, s32[2,128,128]{2,1,0:T(8,128)} %bitcast.10, s32[2,1,1,2]{3,2,1,0:T(1,128)} %bitcast.11, f32[5,128,128]{2,1,0:T(8,128)} %constant.2.clone.table), custom_call_target="tpu_custom_call" | custom-call | flops 7000000000 | bytes 2000000 | tf_op jit(solution)/shard_map/crossing/pallas_call | solution.py:483
  29.8 1.0 %finish.1 = (f32[2,5,128,128]{3,2,1,0:T(8,128)}, f32[2,5,64,128]{3,2,1,0:T(8,128)}) custom-call(f32[2,5,128,128]{3,2,1,0:T(8,128)S(1)} %get-tuple-element.7.kept_in, f32[2,5,64,128]{3,2,1,0:T(8,128)S(1)} %get-tuple-element.8.arrived, f32[2,2,64,128]{3,2,1,0:T(8,128)S(1)} %get-tuple-element.9.arrived_kicks), custom_call_target="tpu_custom_call" | custom-call | tf_op jit(solution)/shard_map/finish/pallas_call | solution.py:529

commit v8 on v7

--- a/solution.py
+++ b/solution.py
@@ -253,7 +253,7 @@
                 behind(distance * (1 - 2 * beam)),
                 dom,
             )
-            for distance in (2, 3, 1)
+            for distance in (1, 3, 2)
         ]
 
     def share_copy(beam):

time: 31 us -> 30.7 us (level)
  no operation moved by 1% of the time
where the time goes in v8:
time: 30.7 us; the launch traced here: 30.6 us
  Pallas kernels  29.9 us (97%)
  between operations  0.64 us (2%)
    pallas_call x1, Pallas kernels, local(): pl.pallas_call(functools.partial(kernel, slices), out_shape=(*shapes, jax...  28.9 us
    pallas_call x1, Pallas kernels, local(): pl.pallas_call(finish, out_shape=shapes, in_specs=[in_vmem, in_vmem, in_v...  1.02 us

profile of v8, /device:TPU:1, one launch (start us, length us, event | category | flops | bytes accessed | tf_op | source)
XLA Modules:
  0.0 30.6 jit_solution(6454363978047313129)
XLA Ops:
  0.6 28.9 %crossing.1 = (f32[2,5,128,128]{3,2,1,0:T(8,128)S(1)}, f32[2,5,64,128]{3,2,1,0:T(8,128)S(1)}, f32[2,2,64,128]{3,2,1,0:T(8,128)S(1)}) custom-call(f32[2,5,128,128]{3,2,1,0:T(8,128)} %bitcast.7, s32[2,128,128]{2,1,0:T(8,128)} %bitcast.10, s32[2,1,1,2]{3,2,1,0:T(1,128)} %bitcast.11, f32[5,128,128]{2,1,0:T(8,128)} %constant.2.clone.table), custom_call_target="tpu_custom_call" | custom-call | flops 7000000000 | bytes 2000000 | tf_op jit(solution)/shard_map/crossing/pallas_call | solution.py:483
  29.5 1.0 %finish.1 = (f32[2,5,128,128]{3,2,1,0:T(8,128)}, f32[2,5,64,128]{3,2,1,0:T(8,128)}) custom-call(f32[2,5,128,128]{3,2,1,0:T(8,128)S(1)} %get-tuple-element.7.kept_in, f32[2,5,64,128]{3,2,1,0:T(8,128)S(1)} %get-tuple-element.8.arrived, f32[2,2,64,128]{3,2,1,0:T(8,128)S(1)} %get-tuple-element.9.arrived_kicks), custom_call_target="tpu_custom_call" | custom-call | tf_op jit(solution)/shard_map/finish/pallas_call | solution.py:529

commit v9 on v8

--- a/solution.py
+++ b/solution.py
@@ -253,7 +253,7 @@
                 behind(distance * (1 - 2 * beam)),
                 dom,
             )
-            for distance in (1, 3, 2)
+            for distance in (3, 1, 2)
         ]
 
     def share_copy(beam):

time: 30.7 us -> 31.3 us (1.020)
  Pallas kernels: 29.9 us -> 30.5 us
    pallas_call x1, Pallas kernels: 28.9 us -> 29.5 us  [local(): pl.pallas_call(functools.partial(kernel, slices), out_shape=(*shapes, jax...]
where the time goes in v9:
time: 31.3 us; the launch traced here: 31.2 us
  Pallas kernels  30.5 us (97%)
  between operations  0.64 us (2%)
    pallas_call x1, Pallas kernels, local(): pl.pallas_call(functools.partial(kernel, slices), out_shape=(*shapes, jax...  29.5 us
    pallas_call x1, Pallas kernels, local(): pl.pallas_call(finish, out_shape=shapes, in_specs=[in_vmem, in_vmem, in_v...  1.02 us

profile of v9, /device:TPU:1, one launch (start us, length us, event | category | flops | bytes accessed | tf_op | source)
XLA Modules:
  0.0 31.2 jit_solution(7189531963401716485)
XLA Ops:
  0.6 29.5 %crossing.1 = (f32[2,5,128,128]{3,2,1,0:T(8,128)S(1)}, f32[2,5,64,128]{3,2,1,0:T(8,128)S(1)}, f32[2,2,64,128]{3,2,1,0:T(8,128)S(1)}) custom-call(f32[2,5,128,128]{3,2,1,0:T(8,128)} %bitcast.7, s32[2,128,128]{2,1,0:T(8,128)} %bitcast.10, s32[2,1,1,2]{3,2,1,0:T(1,128)} %bitcast.11, f32[5,128,128]{2,1,0:T(8,128)} %constant.2.clone.table), custom_call_target="tpu_custom_call" | custom-call | flops 7000000000 | bytes 2000000 | tf_op jit(solution)/shard_map/crossing/pallas_call | solution.py:483
  30.1 1.0 %finish.1 = (f32[2,5,128,128]{3,2,1,0:T(8,128)}, f32[2,5,64,128]{3,2,1,0:T(8,128)}) custom-call(f32[2,5,128,128]{3,2,1,0:T(8,128)S(1)} %get-tuple-element.7.kept_in, f32[2,5,64,128]{3,2,1,0:T(8,128)S(1)} %get-tuple-element.8.arrived, f32[2,2,64,128]{3,2,1,0:T(8,128)S(1)} %get-tuple-element.9.arrived_kicks), custom_call_target="tpu_custom_call" | custom-call | tf_op jit(solution)/shard_map/finish/pallas_call | solution.py:529
